TPU v7x, 256 devices: a whole 4x4x8 slice. The times are simulated.
256 devices in a mesh: row: 8 (over x, core), feat: 32 (over y, z).
Axes of the slice: x: 4, y: 4, z: 8, core: 2. Of those that a mesh axis runs over, the one named last changes fastest.
Arguments:
- doc_scores: float32 [262144], P(('row', 'feat')), may hold values from -8 to 8
- doc_labels: int32 [262144], P(('row', 'feat')), may hold values from 0 to 4
- doc_ranks: int32 [262144], P(('row', 'feat')), may hold values from 0 to 1023, as said below
- query_tiles: int32 [8, 64], P('row'), may hold values from 1 to 8, as said below
- bin_codes: int32 [2048, 262144], P('feat', 'row'), may hold values from 0 to 255
Outputs:
- gradient: float32 [262144], P(('row', 'feat'))
- hessian: float32 [262144], P(('row', 'feat'))
- histogram: float32 [2048, 2, 256], P('feat')
- split_gain: float32 [2048], P('feat')
Inputs may be any that keep to these rules, and one draw needn't show every extreme that they name: `query_tiles`: in every slab the counts sum to 256; every slab has at least one query of 1 tile and one of 8 tiles. `doc_ranks`: within a query of c tiles the ranks of its documents are 0 to 128 c - 1, each once.
All inputs are finite; a program needn't handle non-finite values.
Results may differ from a plain program's by a relative error of at most 0.0045.
Values may be sent and summed in bfloat16 or wider, within the bound.
A program may use at most 64 MiB of HBM per device.

v0:
```python
import jax
import jax.numpy as jnp
from jax import lax
from jax.sharding import PartitionSpec as P

BINS = 256
MAX_TILES = 8


LEVEL_GAINS = (0.0, 1.0, 3.0, 7.0, 15.0)


def gain_of(labels_in):
    totals = jnp.zeros(labels_in.shape, jnp.float32)
    for level in range(5):
        totals = totals + jnp.where(
            labels_in == level, jnp.float32(LEVEL_GAINS[level]), jnp.float32(0.0)
        )
    return totals


def disc_of(ranks_in):
    return 1.0 / jnp.log2(ranks_in.astype(jnp.float32) + 2.0)


def prefix_table(longest):
    places = jnp.arange(longest, dtype=jnp.int32).astype(jnp.float32)
    values = 1.0 / jnp.log2(places + 2.0)
    return jnp.concatenate([jnp.zeros((1,), jnp.float32), jnp.cumsum(values)])


def lookup(table, where_float):
    places = jnp.arange(table.shape[0], dtype=jnp.int32).astype(jnp.float32)
    equal = places == where_float[..., None]
    return jnp.sum(jnp.where(equal, table, jnp.float32(0.0)), axis=-1)


def query_norms(gains, sizes, starts, longest):
    count_docs = gains.shape[0]
    positions = jnp.arange(count_docs, dtype=jnp.int32)
    query_ids = jnp.sum((positions[None, :] >= starts[:, None]).astype(jnp.int32), axis=0) - 1
    member = (query_ids[None, :] == jnp.arange(sizes.shape[0], dtype=jnp.int32)[:, None]).astype(
        jnp.bfloat16
    )
    levels = jnp.array(LEVEL_GAINS, jnp.float32)
    level_hot = (gains[:, None] == levels[None, :]).astype(jnp.bfloat16)
    counts = jnp.dot(member, level_hot, preferred_element_type=jnp.float32)
    upper = (
        jnp.arange(5, dtype=jnp.int32)[None, :] > jnp.arange(5, dtype=jnp.int32)[:, None]
    ).astype(jnp.float32)
    higher = jnp.sum(counts[:, None, :] * upper[None, :, :], axis=2)
    table = prefix_table(longest)
    ideal = jnp.sum(
        levels[None, :] * (lookup(table, higher + counts) - lookup(table, higher)), axis=1
    )
    return 1.0 + ideal


def pair_sums(score_row, gain_row, disc_row, score_col, gain_col, disc_col, norm_value):
    diff = score_row[:, None] - score_col[None, :]
    weight = (
        jnp.abs(gain_row[:, None] - gain_col[None, :])
        * jnp.abs(disc_row[:, None] - disc_col[None, :])
        / norm_value
    )
    rising = jax.nn.sigmoid(diff)
    falling = jax.nn.sigmoid(-diff)
    zeroes = jnp.zeros_like(weight)
    terms = jnp.where(
        gain_row[:, None] > gain_col[None, :],
        -weight * falling,
        jnp.where(gain_row[:, None] < gain_col[None, :], weight * rising, zeroes),
    )
    return (jnp.sum(terms, axis=1), jnp.sum(weight * rising * falling, axis=1))


def best_gains(hist):
    running = jnp.cumsum(hist, axis=2)
    grad_left = running[:, 0, :-1]
    hess_left = running[:, 1, :-1]
    grad_all = running[:, 0, -1:]
    hess_all = running[:, 1, -1:]
    grad_right = grad_all - grad_left
    gains = (
        grad_left * grad_left / (hess_left + 1.0)
        + grad_right * grad_right / (hess_all - hess_left + 1.0)
        - grad_all * grad_all / (hess_all + 1.0)
    )
    return jnp.max(gains, axis=1)


def shards(doc_scores, doc_labels, doc_ranks, query_tiles, bin_codes):
    feat_count = lax.axis_size("feat")
    feat_index = lax.axis_index("feat")
    half_turn = feat_count // 2
    doc_local = doc_scores.shape[0]
    gains_local = gain_of(doc_labels)
    discs_local = disc_of(doc_ranks)
    slab_scores, slab_gains, slab_discs = (
        lax.all_gather(doc_scores, "feat", axis=0, tiled=True),
        lax.all_gather(gains_local, "feat", axis=0, tiled=True),
        lax.all_gather(discs_local, "feat", axis=0, tiled=True),
    )
    slab_docs = slab_scores.shape[0]
    longest = MAX_TILES * 128
    tile_sizes = query_tiles[0]
    sizes = tile_sizes * 128
    starts = jnp.cumsum(sizes) - sizes
    norms = query_norms(slab_gains, sizes, starts, longest)
    tile_count = slab_docs // 128
    tile_first = jnp.arange(tile_count, dtype=jnp.int32) * 128
    select = (tile_first[:, None] >= starts[None, :]) & (
        tile_first[:, None] < (starts + sizes)[None, :]
    )
    select_int = select.astype(jnp.int32)
    before = jnp.cumsum(tile_sizes) - tile_sizes
    owner = (before * feat_count // jnp.sum(tile_sizes) + half_turn) % feat_count
    tile_owner = jnp.sum(select_int * owner[None, :], axis=1)
    tile_start = jnp.sum(select_int * starts[None, :], axis=1)
    tile_span = jnp.sum(select_int * tile_sizes[None, :], axis=1)
    tile_norm = jnp.sum(jnp.where(select, norms[None, :], jnp.float32(0.0)), axis=1)
    owned = (tile_owner == feat_index).astype(jnp.int32)
    place = jnp.cumsum(owned) - 1
    tile_ids = jnp.arange(tile_count, dtype=jnp.int32)
    listed = (owned[:, None] == 1) & (place[:, None] == tile_ids[None, :])
    work_list = jnp.sum(jnp.where(listed, tile_ids[:, None], 0), axis=0)
    busy_tiles = jnp.sum(owned)

    def row_tile(position, carried):
        tile = work_list[position]
        begin = tile * 128
        score_row = lax.dynamic_slice_in_dim(slab_scores, begin, 128)
        gain_row = lax.dynamic_slice_in_dim(slab_gains, begin, 128)
        disc_row = lax.dynamic_slice_in_dim(slab_discs, begin, 128)
        query_begin = tile_start[tile]
        norm_value = tile_norm[tile]

        def col_tile(column, sums):
            column_begin = query_begin + column * 128
            score_col = lax.dynamic_slice_in_dim(slab_scores, column_begin, 128)
            gain_col = lax.dynamic_slice_in_dim(slab_gains, column_begin, 128)
            disc_col = lax.dynamic_slice_in_dim(slab_discs, column_begin, 128)
            grads, hessians = pair_sums(
                score_row, gain_row, disc_row, score_col, gain_col, disc_col, norm_value
            )
            return (sums[0] + grads, sums[1] + hessians)

        empty_row = jnp.zeros((128,), jnp.float32)
        grads, hessians = lax.fori_loop(0, tile_span[tile], col_tile, (empty_row, empty_row))
        return lax.dynamic_update_slice(
            carried, jnp.stack([grads, hessians]), (jnp.int32(0), begin)
        )

    owned_lambdas = lax.fori_loop(0, busy_tiles, row_tile, jnp.zeros((2, slab_docs), jnp.float32))
    summed = lax.psum(owned_lambdas, "feat")
    mine = lax.dynamic_slice(summed, (jnp.int32(0), feat_index * doc_local), (2, doc_local))
    slab_lambdas = summed.astype(jnp.bfloat16)
    gradient = mine[0]
    hessian = mine[1]
    feat_local = bin_codes.shape[0]
    block_count = 16
    block_rows = slab_docs // block_count
    bin_ids = jnp.arange(BINS, dtype=jnp.int32)

    def add_block(block_index, running):
        code_block = lax.dynamic_slice_in_dim(bin_codes, block_index * block_rows, block_rows, 1)
        bin_hot = (code_block[:, :, None] == bin_ids[None, None, :]).astype(jnp.bfloat16)
        lambda_block = lax.dynamic_slice_in_dim(
            slab_lambdas, block_index * block_rows, block_rows, 1
        )
        return running + jnp.einsum(
            "cr,frb->fcb", lambda_block, bin_hot, preferred_element_type=jnp.float32
        )

    partial_hist = lax.fori_loop(
        0, block_count, add_block, jnp.zeros((feat_local, 2, BINS), jnp.float32)
    )
    histogram = lax.psum(partial_hist, "row")
    best = best_gains(histogram)
    largest = lax.pmax(jnp.max(best), "feat")
    split_gain = best / (largest + 1e-06)
    return (gradient, hessian, histogram, split_gain)


def solution(mesh):
    return jax.shard_map(
        shards,
        mesh=mesh,
        in_specs=(
            P(("row", "feat")),
            P(("row", "feat")),
            P(("row", "feat")),
            P("row", None),
            P("feat", "row"),
        ),
        out_specs=(P(("row", "feat")), P(("row", "feat")), P("feat", None, None), P("feat")),
        check_vma=False,
    )
```

profile of v0, /device:TPU:1, one launch (start us, length us, event | category | flops | bytes accessed | tf_op | source)
XLA Modules:
  0.0 1292.0 jit_solution(14868734871373563078)
XLA Ops:
  14.5 37.3 %all_gather.9 = f32[32768]{0:T(1024)S(1)} all-gather(f32[1024]{0:T(1024)} %param.12), channel_id=1, replica_groups=mesh['row'=8,'feat'=32] {'feat'}, dimensions={0}, use_global_device_ids=true | all-gather | bytes 135168 | tf_op jit(solution)/shard_map/all_gather | solution.py:100
  52.5 32.3 %all_gather.10 = f32[32768]{0:T(1024)S(1)} all-gather(f32[1024]{0:T(1024)S(1)} %select_add_fusion), channel_id=1, replica_groups=mesh['row'=8,'feat'=32] {'feat'}, dimensions={0}, use_global_device_ids=true | all-gather | bytes 135168 | tf_op jit(solution)/shard_map/all_gather | solution.py:101
  85.5 31.4 %all_gather.11 = f32[32768]{0:T(1024)S(1)} all-gather(f32[1024]{0:T(1024)S(1)} %multiply_divide_fusion.2), channel_id=1, replica_groups=mesh['row'=8,'feat'=32] {'feat'}, dimensions={0}, use_global_device_ids=true | all-gather | bytes 135168 | tf_op jit(solution)/shard_map/all_gather | solution.py:102
  122.7 175.2 %while.37 = (s32[]{:T(128)}, f32[2,32768]{1,0:T(2,128)S(1)}, s32[]{:T(128)}, s32[256]{0:T(256)S(1)}, s32[256]{0:T(256)S(1)}, /*index=5*/s32[256]{0:T(256)S(1)}, ...) while((s32[]{:T(128)}, f32[2,32768]{1,0:T(2,128)S(1)}, ...), condition=%wide.region_23.24_spmd, body=%wide.region_18.23_spmd.sunk | while | flops 360723 | bytes 17126 | solution.py:154
  298.8 321.1 %all-reduce.3.cloned.1.call-done = f32[2,32768]{1,0:T(2,128)} async-done(((f32[2,32768]{1,0:T(2,128)}), f32[2,32768]{1,0:T(2,128)}) %all-reduce.3.cloned.1.call-update) | async-done | bytes 262160 | tf_op jit(solution)/shard_map/psum | solution.py:155
  620.9 531.8 %while.38 = (s32[]{:T(128)}, f32[64,2,256]{2,1,0:T(2,128)S(1)}, s32[64,32768]{1,0:T(8,128)}, bf16[2,32768]{1,0:T(2,128)(2,1)S(1)}, s32[]{:T(128)}, /*index=5*/s32[]{:T(128)}, s32[]{:T(128)}, s32[]{:T(128)}) while((s32[]{:T(128)}, f32[64,2,256]{2,1,0:T(2,128)S(1)}, s32[64,32768]{1,0:T(8,128)}, bf16[2,32768]{1,0:T(2,128)(2,1)S(1)}, ...), condition=%wide.region_26.27_spmd.clone, body=%wide.region_25.26_spmd.clone.sunk | while | flops 167837696 | bytes 1843357 | solution.py:175
  622.0 32.1 %fusion.37 = f32[64,2,256]{2,1,0:T(2,128)S(1)} fusion(s32[64,2048]{1,0:T(8,128)S(1)} %constant_dynamic-slice_fusion.3, f32[64,2,256]{2,1,0:T(2,128)S(1)} %get-tuple-element.616, pred[]{:T(512)S(6)} %compare.4, bf16[2,32768]{1,0:T(2,128)(2,1)S(1)} %get-tuple-element.626, s32[]{:T(128)S(6)} %select_n.116), kind=kOutput, calls=%fused_computation.17.clone.3 | convolution fusion | flops 167837696 | bytes 794629 | tf_op jit(solution)/shard_map/while/body/eval_jaxpr/cr,frb->fcb/dot_general | solution.py:171
  655.2 32.1 %fusion.37 = f32[64,2,256]{2,1,0:T(2,128)S(1)} fusion(s32[64,2048]{1,0:T(8,128)S(1)} %constant_dynamic-slice_fusion.3, f32[64,2,256]{2,1,0:T(2,128)S(1)} %get-tuple-element.616, pred[]{:T(512)S(6)} %compare.4, bf16[2,32768]{1,0:T(2,128)(2,1)S(1)} %get-tuple-element.626, s32[]{:T(128)S(6)} %select_n.116), kind=kOutput, calls=%fused_computation.17.clone.3 | convolution fusion | flops 167837696 | bytes 794629 | tf_op jit(solution)/shard_map/while/body/eval_jaxpr/cr,frb->fcb/dot_general | solution.py:171
  688.5 32.1 %fusion.37 = f32[64,2,256]{2,1,0:T(2,128)S(1)} fusion(s32[64,2048]{1,0:T(8,128)S(1)} %constant_dynamic-slice_fusion.3, f32[64,2,256]{2,1,0:T(2,128)S(1)} %get-tuple-element.616, pred[]{:T(512)S(6)} %compare.4, bf16[2,32768]{1,0:T(2,128)(2,1)S(1)} %get-tuple-element.626, s32[]{:T(128)S(6)} %select_n.116), kind=kOutput, calls=%fused_computation.17.clone.3 | convolution fusion | flops 167837696 | bytes 794629 | tf_op jit(solution)/shard_map/while/body/eval_jaxpr/cr,frb->fcb/dot_general | solution.py:171
  721.7 32.1 %fusion.37 = f32[64,2,256]{2,1,0:T(2,128)S(1)} fusion(s32[64,2048]{1,0:T(8,128)S(1)} %constant_dynamic-slice_fusion.3, f32[64,2,256]{2,1,0:T(2,128)S(1)} %get-tuple-element.616, pred[]{:T(512)S(6)} %compare.4, bf16[2,32768]{1,0:T(2,128)(2,1)S(1)} %get-tuple-element.626, s32[]{:T(128)S(6)} %select_n.116), kind=kOutput, calls=%fused_computation.17.clone.3 | convolution fusion | flops 167837696 | bytes 794629 | tf_op jit(solution)/shard_map/while/body/eval_jaxpr/cr,frb->fcb/dot_general | solution.py:171
  754.9 32.1 %fusion.37 = f32[64,2,256]{2,1,0:T(2,128)S(1)} fusion(s32[64,2048]{1,0:T(8,128)S(1)} %constant_dynamic-slice_fusion.3, f32[64,2,256]{2,1,0:T(2,128)S(1)} %get-tuple-element.616, pred[]{:T(512)S(6)} %compare.4, bf16[2,32768]{1,0:T(2,128)(2,1)S(1)} %get-tuple-element.626, s32[]{:T(128)S(6)} %select_n.116), kind=kOutput, calls=%fused_computation.17.clone.3 | convolution fusion | flops 167837696 | bytes 794629 | tf_op jit(solution)/shard_map/while/body/eval_jaxpr/cr,frb->fcb/dot_general | solution.py:171
  788.2 32.1 %fusion.37 = f32[64,2,256]{2,1,0:T(2,128)S(1)} fusion(s32[64,2048]{1,0:T(8,128)S(1)} %constant_dynamic-slice_fusion.3, f32[64,2,256]{2,1,0:T(2,128)S(1)} %get-tuple-element.616, pred[]{:T(512)S(6)} %compare.4, bf16[2,32768]{1,0:T(2,128)(2,1)S(1)} %get-tuple-element.626, s32[]{:T(128)S(6)} %select_n.116), kind=kOutput, calls=%fused_computation.17.clone.3 | convolution fusion | flops 167837696 | bytes 794629 | tf_op jit(solution)/shard_map/while/body/eval_jaxpr/cr,frb->fcb/dot_general | solution.py:171
  821.4 32.1 %fusion.37 = f32[64,2,256]{2,1,0:T(2,128)S(1)} fusion(s32[64,2048]{1,0:T(8,128)S(1)} %constant_dynamic-slice_fusion.3, f32[64,2,256]{2,1,0:T(2,128)S(1)} %get-tuple-element.616, pred[]{:T(512)S(6)} %compare.4, bf16[2,32768]{1,0:T(2,128)(2,1)S(1)} %get-tuple-element.626, s32[]{:T(128)S(6)} %select_n.116), kind=kOutput, calls=%fused_computation.17.clone.3 | convolution fusion | flops 167837696 | bytes 794629 | tf_op jit(solution)/shard_map/while/body/eval_jaxpr/cr,frb->fcb/dot_general | solution.py:171
  854.6 32.1 %fusion.37 = f32[64,2,256]{2,1,0:T(2,128)S(1)} fusion(s32[64,2048]{1,0:T(8,128)S(1)} %constant_dynamic-slice_fusion.3, f32[64,2,256]{2,1,0:T(2,128)S(1)} %get-tuple-element.616, pred[]{:T(512)S(6)} %compare.4, bf16[2,32768]{1,0:T(2,128)(2,1)S(1)} %get-tuple-element.626, s32[]{:T(128)S(6)} %select_n.116), kind=kOutput, calls=%fused_computation.17.clone.3 | convolution fusion | flops 167837696 | bytes 794629 | tf_op jit(solution)/shard_map/while/body/eval_jaxpr/cr,frb->fcb/dot_general | solution.py:171
  887.9 32.1 %fusion.37 = f32[64,2,256]{2,1,0:T(2,128)S(1)} fusion(s32[64,2048]{1,0:T(8,128)S(1)} %constant_dynamic-slice_fusion.3, f32[64,2,256]{2,1,0:T(2,128)S(1)} %get-tuple-element.616, pred[]{:T(512)S(6)} %compare.4, bf16[2,32768]{1,0:T(2,128)(2,1)S(1)} %get-tuple-element.626, s32[]{:T(128)S(6)} %select_n.116), kind=kOutput, calls=%fused_computation.17.clone.3 | convolution fusion | flops 167837696 | bytes 794629 | tf_op jit(solution)/shard_map/while/body/eval_jaxpr/cr,frb->fcb/dot_general | solution.py:171
  921.1 32.1 %fusion.37 = f32[64,2,256]{2,1,0:T(2,128)S(1)} fusion(s32[64,2048]{1,0:T(8,128)S(1)} %constant_dynamic-slice_fusion.3, f32[64,2,256]{2,1,0:T(2,128)S(1)} %get-tuple-element.616, pred[]{:T(512)S(6)} %compare.4, bf16[2,32768]{1,0:T(2,128)(2,1)S(1)} %get-tuple-element.626, s32[]{:T(128)S(6)} %select_n.116), kind=kOutput, calls=%fused_computation.17.clone.3 | convolution fusion | flops 167837696 | bytes 794629 | tf_op jit(solution)/shard_map/while/body/eval_jaxpr/cr,frb->fcb/dot_general | solution.py:171
  954.3 32.1 %fusion.37 = f32[64,2,256]{2,1,0:T(2,128)S(1)} fusion(s32[64,2048]{1,0:T(8,128)S(1)} %constant_dynamic-slice_fusion.3, f32[64,2,256]{2,1,0:T(2,128)S(1)} %get-tuple-element.616, pred[]{:T(512)S(6)} %compare.4, bf16[2,32768]{1,0:T(2,128)(2,1)S(1)} %get-tuple-element.626, s32[]{:T(128)S(6)} %select_n.116), kind=kOutput, calls=%fused_computation.17.clone.3 | convolution fusion | flops 167837696 | bytes 794629 | tf_op jit(solution)/shard_map/while/body/eval_jaxpr/cr,frb->fcb/dot_general | solution.py:171
  987.6 32.1 %fusion.37 = f32[64,2,256]{2,1,0:T(2,128)S(1)} fusion(s32[64,2048]{1,0:T(8,128)S(1)} %constant_dynamic-slice_fusion.3, f32[64,2,256]{2,1,0:T(2,128)S(1)} %get-tuple-element.616, pred[]{:T(512)S(6)} %compare.4, bf16[2,32768]{1,0:T(2,128)(2,1)S(1)} %get-tuple-element.626, s32[]{:T(128)S(6)} %select_n.116), kind=kOutput, calls=%fused_computation.17.clone.3 | convolution fusion | flops 167837696 | bytes 794629 | tf_op jit(solution)/shard_map/while/body/eval_jaxpr/cr,frb->fcb/dot_general | solution.py:171
  1020.8 32.1 %fusion.37 = f32[64,2,256]{2,1,0:T(2,128)S(1)} fusion(s32[64,2048]{1,0:T(8,128)S(1)} %constant_dynamic-slice_fusion.3, f32[64,2,256]{2,1,0:T(2,128)S(1)} %get-tuple-element.616, pred[]{:T(512)S(6)} %compare.4, bf16[2,32768]{1,0:T(2,128)(2,1)S(1)} %get-tuple-element.626, s32[]{:T(128)S(6)} %select_n.116), kind=kOutput, calls=%fused_computation.17.clone.3 | convolution fusion | flops 167837696 | bytes 794629 | tf_op jit(solution)/shard_map/while/body/eval_jaxpr/cr,frb->fcb/dot_general | solution.py:171
  1054.0 32.1 %fusion.37 = f32[64,2,256]{2,1,0:T(2,128)S(1)} fusion(s32[64,2048]{1,0:T(8,128)S(1)} %constant_dynamic-slice_fusion.3, f32[64,2,256]{2,1,0:T(2,128)S(1)} %get-tuple-element.616, pred[]{:T(512)S(6)} %compare.4, bf16[2,32768]{1,0:T(2,128)(2,1)S(1)} %get-tuple-element.626, s32[]{:T(128)S(6)} %select_n.116), kind=kOutput, calls=%fused_computation.17.clone.3 | convolution fusion | flops 167837696 | bytes 794629 | tf_op jit(solution)/shard_map/while/body/eval_jaxpr/cr,frb->fcb/dot_general | solution.py:171
  1087.3 32.1 %fusion.37 = f32[64,2,256]{2,1,0:T(2,128)S(1)} fusion(s32[64,2048]{1,0:T(8,128)S(1)} %constant_dynamic-slice_fusion.3, f32[64,2,256]{2,1,0:T(2,128)S(1)} %get-tuple-element.616, pred[]{:T(512)S(6)} %compare.4, bf16[2,32768]{1,0:T(2,128)(2,1)S(1)} %get-tuple-element.626, s32[]{:T(128)S(6)} %select_n.116), kind=kOutput, calls=%fused_computation.17.clone.3 | convolution fusion | flops 167837696 | bytes 794629 | tf_op jit(solution)/shard_map/while/body/eval_jaxpr/cr,frb->fcb/dot_general | solution.py:171
  1120.5 32.1 %fusion.37 = f32[64,2,256]{2,1,0:T(2,128)S(1)} fusion(s32[64,2048]{1,0:T(8,128)S(1)} %constant_dynamic-slice_fusion.3, f32[64,2,256]{2,1,0:T(2,128)S(1)} %get-tuple-element.616, pred[]{:T(512)S(6)} %compare.4, bf16[2,32768]{1,0:T(2,128)(2,1)S(1)} %get-tuple-element.626, s32[]{:T(128)S(6)} %select_n.116), kind=kOutput, calls=%fused_computation.17.clone.3 | convolution fusion | flops 167837696 | bytes 794629 | tf_op jit(solution)/shard_map/while/body/eval_jaxpr/cr,frb->fcb/dot_general | solution.py:171
  1154.8 62.3 %all-reduce.5.cloned.1.call-done = f32[64,2,256]{2,1,0:T(2,128)} async-done(((f32[64,2,256]{2,1,0:T(2,128)}), f32[64,2,256]{2,1,0:T(2,128)}) %all-reduce.5.cloned.1.call-update) | async-done | bytes 131088 | tf_op jit(solution)/shard_map/psum | solution.py:178
  1220.7 61.8 %pmax.7 = f32[]{:T(128)} all-reduce(f32[]{:T(128)} %get-tuple-element.238), channel_id=1, replica_groups=mesh['row'=8,'feat'=32] {'feat'}, use_global_device_ids=true, to_apply=%region_32.33 | all-reduce | flops 1 | bytes 8 | tf_op jit(solution)/shard_map/pmax | solution.py:180
  (458 shorter events, 222.7 us)
Async XLA Ops:
  7.2 612.7 %all-reduce.3.cloned.1.call-start = ((), (), s32[]{:S(2)}) async-start(), calls=%async_computation | async-start | bytes 524288 | tf_op jit(solution)/shard_map/psum | solution.py:155
  298.0 0.7 copy-start
  298.7 918.4 %all-reduce.5.cloned.1.call-start = ((), (), s32[]{:S(2)}) async-start(), calls=%async_computation.1 | async-start | bytes 262144 | tf_op jit(solution)/shard_map/psum | solution.py:178
  1152.7 0.7 copy-start.1
Sparse Core Ops, SparseCore 0:
  298.8 320.9 all-reduce.2
  1153.5 63.5 all-reduce.4
where the time goes:
time: 1310 us; the launch traced here: 1290 us
  matrix products  517 us (39%)
  waiting for transfers between devices  383 us (29%)
  blocking collectives  163 us (12%)
  loops' own time  103 us (8%)
  local copies, waits for them, and re-layouts  62.6 us (5%)
  other arithmetic  48.3 us (4%)
  between operations  15.5 us (1%)
    dot_general x16, matrix products, add_block(): jnp.einsum('cr,frb->fcb', lambda_block, bin_hot, preferred_element_type=j...  514 us
    psum x1, waiting for transfers between devices, shards(): summed = lax.psum(owned_lambdas, 'feat')  321 us
    another operation x11, loops' own time, row_tile(): lax.fori_loop(0, tile_span[tile], col_tile, (empty_row, empty_row))  65.9 us
    psum x1, waiting for transfers between devices, shards(): histogram = lax.psum(partial_hist, 'row')  62.3 us
    pmax x1, blocking collectives, shards(): largest = lax.pmax(jnp.max(best), 'feat')  61.8 us
    all_gather x1, blocking collectives, shards(): lax.all_gather(doc_scores, 'feat', axis=0, tiled=True)  37.3 us
    another operation x1, loops' own time, shards(): lax.fori_loop(0, busy_tiles, row_tile, jnp.zeros((2, slab_docs), jnp.floa...  36.7 us
    reduce_sum x43, other arithmetic, pair_sums(): return (jnp.sum(terms, axis=1), jnp.sum(weight * rising * falling, axis=1))  32.6 us
  transfers between devices with their start and end apart: 2, of which 2 were waited for; matrix products, arithmetic and copies ran while one was open for 0% of the time, Pallas kernels for 0%

commit v1 on v0

v1 whole, which is shorter than its diff:
```python
import functools

import jax
import jax.experimental.pallas as pl
import jax.experimental.pallas.tpu as pltpu
import jax.numpy as jnp
from jax import lax
from jax.sharding import PartitionSpec as P

BINS = 256
MAX_TILES = 8
LANES = 128
QUERIES = 64
HIGH, LOW = 8, 32
GROUP = 8
MESH = pl.DeviceIdType.MESH
F32, BF16, F8, I8 = jnp.float32, jnp.bfloat16, jnp.float8_e4m3fn, jnp.int8


def iota(shape, dim):
    return lax.broadcasted_iota(jnp.int32, shape, dim)


def pieces(x):
    first = x.astype(BF16)
    rest = x - first.astype(F32)
    second = rest.astype(BF16)
    third = (rest - second.astype(F32)).astype(BF16)
    return first, second, third


def lambda_kernel(feats, tiles_ref, score_ref, label_ref, rank_ref, grad_ref, hess_ref, all_ref,
                  window, wide, sums, gathered, halo_send, halo_recv, send, recv):
    me = lax.axis_index("feat")
    left, right = lax.rem(me + feats - 1, feats), lax.rem(me + 1, feats)
    barrier = pltpu.get_barrier_semaphore()

    @pl.loop(1, feats)
    def _(step):
        pl.semaphore_signal(barrier, inc=1, device_id={"feat": lax.rem(me + step, feats)}, device_id_type=MESH)

    odds = jnp.exp(score_ref[...])
    gains = (jnp.left_shift(1, label_ref[...]) - 1).astype(F32)
    discs = 1.0 / jnp.log2(rank_ref[...].astype(F32) + 2.0)
    own = (odds, gains, discs)
    for which in range(3):
        window[which, 8:16, :] = own[which]
    pl.semaphore_wait(barrier, feats - 1)
    halos = []
    for side, (target, place) in enumerate(((left, 16), (right, 0))):
        copy = pltpu.make_async_remote_copy(
            src_ref=window.at[:, pl.ds(8, 8), :], dst_ref=window.at[:, pl.ds(place, 8), :],
            send_sem=halo_send.at[side], recv_sem=halo_recv.at[side],
            device_id={"feat": target}, device_id_type=MESH)
        copy.start()
        halos.append(copy)

    first = [jnp.int32(0)] * 8
    count = [jnp.int32(1)] * 8
    start = 8 - me * 8
    for query in range(QUERIES):
        tiles = tiles_ref[0, query]
        for tile in range(8):
            inside = start <= 8 + tile
            first[tile] = jnp.where(inside, start, first[tile])
            count[tile] = jnp.where(inside, tiles, count[tile])
        start = start + tiles

    for which in range(3):
        turned = jnp.transpose(own[which])
        for tile in range(8):
            wide[which, tile] = jnp.broadcast_to(turned[:, tile:tile + 1], (LANES, LANES))

    place = (iota((8, LANES), 0) * LANES + iota((8, LANES), 1)).astype(F32)
    table = 1.0 / jnp.log2(place + 2.0)
    rows = iota((8, LANES), 0)
    first_rows, count_rows = jnp.zeros((8, LANES), jnp.int32), jnp.zeros((8, LANES), jnp.int32)
    for tile in range(8):
        first_rows = jnp.where(rows == tile, first[tile], first_rows)
        count_rows = jnp.where(rows == tile, count[tile], count_rows)

    for copy in halos:
        copy.wait()

    ones = jnp.ones((LANES, LANES), BF16)
    all_gains = window[1]
    reach = jnp.concatenate([(all_gains >= F32(2 ** level - 1)).astype(F32) for level in range(1, 5)], axis=0)
    reach = jnp.dot(reach.astype(BF16), ones, preferred_element_type=F32)
    above = [jnp.zeros((8, LANES), F32)] * 4
    for tile in range(24):
        member = (first_rows <= tile) & (first_rows + count_rows > tile)
        for level in range(4):
            at = level * 24 + tile
            above[level] = above[level] + jnp.where(member, jnp.broadcast_to(reach[at:at + 1], (8, LANES)), 0.0)
    ideals = []
    for tile in range(8):
        total = jnp.zeros((8, LANES), F32)
        for level in range(4):
            limit = jnp.broadcast_to(above[level][tile:tile + 1], (8, LANES))
            total = total + jnp.where(place < limit, table * F32(2 ** level), 0.0)
        ideals.append(jnp.sum(total, axis=0, keepdims=True))
    ideal = jnp.sum(jnp.concatenate(ideals, axis=0), axis=1, keepdims=True)
    scale = 1.0 / (1.0 + ideal)

    lanes = iota((LANES, LANES), 1)
    totals = jnp.zeros((LANES, LANES), F32)
    for tile in range(8):
        columns = []
        for step in range(MAX_TILES):
            at = jnp.minimum(jnp.maximum(first[tile] + step, 0), 23)
            columns.append([window[which, pl.ds(at, 1), :] for which in range(3)]
                           + [jnp.where(step < count[tile], F32(1), F32(0))])

        @pl.loop(0, LANES // 16)
        def _(part):
            here = pl.ds(pl.multiple_of(part * 16, 16), 16)
            odds_i, gain_i, disc_i = (wide[which, tile, here, :] for which in range(3))
            grad = jnp.zeros((16, LANES), F32)
            hess = jnp.zeros((16, LANES), F32)
            for odds_j, gain_j, disc_j, valid in columns:
                inverse = pl.reciprocal(odds_i + odds_j, approx=True)
                delta = gain_i - gain_j
                weight = delta * (jnp.abs(disc_i - disc_j) * (inverse * valid))
                grad = grad + weight * jnp.where(delta > 0, odds_j, odds_i)
                hess = hess + jnp.abs(weight) * (inverse * odds_j)
            sums[0, here, :] = grad
            sums[1, here, :] = hess

        for which in range(2):
            high = sums[which].astype(BF16)
            low = (sums[which] - high.astype(F32)).astype(BF16)
            added = (jnp.dot(high, ones, preferred_element_type=F32)
                     + jnp.dot(low, ones, preferred_element_type=F32))
            totals = jnp.where(lanes == which * 8 + tile, added, totals)
    totals = jnp.transpose(totals)
    gradient = -totals[0:8] * scale
    hessian = totals[8:16] * (odds * scale)
    grad_ref[...] = gradient
    hess_ref[...] = hessian
    gathered[me] = jnp.concatenate([gradient, hessian], axis=0).astype(BF16)

    def exchange(step):
        target = lax.rem(me + step, feats)
        return pltpu.make_async_remote_copy(
            src_ref=gathered.at[me], dst_ref=gathered.at[me], send_sem=send.at[step], recv_sem=recv.at[step],
            device_id={"feat": target}, device_id_type=MESH)

    @pl.loop(1, feats)
    def _(step):
        exchange(step).start()

    @pl.loop(1, feats)
    def _(step):
        exchange(step).wait()

    all_ref[...] = gathered[...]


def lambdas(feats, tiles, scores, labels, ranks):
    block = jax.ShapeDtypeStruct((8, LANES), F32)
    vmem = pl.BlockSpec(memory_space=pltpu.VMEM)
    return pl.pallas_call(
        functools.partial(lambda_kernel, feats),
        out_shape=(block, block, jax.ShapeDtypeStruct((feats, 16, LANES), BF16)),
        in_specs=[pl.BlockSpec(memory_space=pltpu.SMEM), vmem, vmem, vmem],
        out_specs=(vmem, vmem, vmem),
        scratch_shapes=[
            pltpu.VMEM((3, 24, LANES), F32), pltpu.VMEM((3, 8, LANES, LANES), F32), pltpu.VMEM((2, LANES, LANES), F32),
            pltpu.VMEM((feats, 16, LANES), BF16),
            pltpu.SemaphoreType.DMA((2,)), pltpu.SemaphoreType.DMA((2,)),
            pltpu.SemaphoreType.DMA((feats,)), pltpu.SemaphoreType.DMA((feats,)),
        ],
        compiler_params=pltpu.CompilerParams(collective_id=0, has_side_effects=True, vmem_limit_bytes=32 * 2 ** 20),
        name="lambdas",
    )(tiles, scores, labels, ranks)


def histogram_kernel(groups, docs, unroll, lam_ref, codes_ref, out_ref, codes, spread, sems):
    def fetch(group):
        slot = lax.rem(group, 3)
        return pltpu.make_async_copy(
            codes_ref.at[pl.ds(pl.multiple_of(group * GROUP, GROUP), GROUP), :], codes.at[slot], sems.at[slot])

    for group in range(3):
        fetch(group).start()

    @pl.loop(0, docs // 1024)
    def _(owner):
        part = lam_ref[owner].astype(F32)
        for which in range(2):
            for tile in range(8):
                at = pl.ds(pl.multiple_of(owner * 1024 + tile * LANES, LANES), LANES)
                row = which * 8 + tile
                spread[which, :, at] = jnp.broadcast_to(part[row:row + 1], (16, LANES)).astype(BF16)

    def body(*accs):
        zero = jnp.zeros((), BF16)

        @pl.loop(0, groups)
        def _(group):
            fetch(group).wait()
            slot = lax.rem(group, 3)

            def one(chunk, acc, mxu):
                at = pl.ds(pl.multiple_of(chunk * BINS, BINS), BINS)
                code = codes[slot, :, at]
                high = (code >> 5).astype(F32)
                high = jnp.concatenate([high, high - 1.0], axis=0).astype(BF16)
                hits = [high == jnp.array(2 * k, BF16) for k in range(HIGH // 2)]
                lhs = jnp.concatenate(
                    [jnp.where(hit, spread[which, :, at], zero) for which in range(2) for hit in hits], axis=0)
                low = code & (LOW - 1)
                low = jnp.concatenate([low - k for k in range(4)], axis=0).astype(I8)
                rhs = jnp.concatenate(
                    [jnp.where(low == jnp.array(4 * k, I8), jnp.ones((), F8), jnp.zeros((), F8)) for k in range(LOW // 4)],
                    axis=0)
                pltpu.matmul_push_rhs(rhs, 0, mxu, transpose=True)
                pltpu.matmul_acc_lhs(acc, lhs, load_staged_rhs=0)

            half = docs // BINS // 2

            @pl.loop(0, half // unroll)
            def _(turn):
                for k in range(unroll):
                    for mxu in range(2):
                        one(mxu * half + turn * unroll + k, accs[mxu], mxu)

            @pl.when(group + 3 < groups)
            def _():
                fetch(group + 3).start()

            total = (pltpu.matmul_pop(accs[0]) + pltpu.matmul_pop(accs[1])).reshape(2 * HIGH, GROUP, BINS)
            shape = (2 * HIGH, GROUP, BINS)
            same = iota(shape, 1) == (iota(shape, 2) & (GROUP - 1))
            out_ref[group] = jnp.sum(jnp.where(same, total, 0.0), axis=1)

    pl.run_scoped(body, *[pltpu.ACC(mxu)((2 * HIGH * GROUP, BINS), F32) for mxu in range(2)])


def histograms(lam, codes, unroll=4):
    feats_here, docs = codes.shape
    groups = feats_here // GROUP
    return pl.pallas_call(
        functools.partial(histogram_kernel, groups, docs, unroll),
        out_shape=jax.ShapeDtypeStruct((groups, 2 * HIGH, BINS), F32),
        in_specs=[pl.BlockSpec(memory_space=pltpu.VMEM), pl.BlockSpec(memory_space=pltpu.HBM)],
        out_specs=pl.BlockSpec(memory_space=pltpu.VMEM),
        scratch_shapes=[
            pltpu.VMEM((3, GROUP, docs), jnp.int32), pltpu.VMEM((2, 16, docs), BF16), pltpu.SemaphoreType.DMA((3,))],
        compiler_params=pltpu.CompilerParams(vmem_limit_bytes=32 * 2 ** 20),
        name="histograms",
    )(lam, codes)


def gain_kernel(rows, feats, part_ref, hist_ref, gain_ref,
                parts, blocks, bests, tops, peaks, send_a, recv_a, send_b, recv_b, send_c, recv_c, send_d, recv_d,
                send_e, recv_e):
    row, feat = lax.axis_index("row"), lax.axis_index("feat")
    barrier = pltpu.get_barrier_semaphore()

    @pl.loop(1, rows)
    def _(step):
        pl.semaphore_signal(barrier, inc=1, device_id={"row": lax.rem(row + step, rows)}, device_id_type=MESH)

    @pl.loop(1, feats)
    def _(step):
        pl.semaphore_signal(barrier, inc=1, device_id={"feat": lax.rem(feat + step, feats)}, device_id_type=MESH)

    source, target = iota((BINS, BINS), 0), iota((BINS, BINS), 1)
    source_low, source_feat = source // GROUP, source % GROUP
    target_feat, target_low = target // LOW, target % LOW
    same = source_feat == target_feat
    as_bf16 = lambda flag: jnp.where(flag, F32(1), F32(0)).astype(BF16)
    move = as_bf16(same & (source_low == target_low))
    prefix = as_bf16(same & (source_low <= target_low))
    whole = as_bf16(same)
    parts[row] = part_ref[row]
    pl.semaphore_wait(barrier, rows + feats - 2)

    def scatter(step):
        to = lax.rem(row + step, rows)
        return pltpu.make_async_remote_copy(
            src_ref=part_ref.at[to], dst_ref=parts.at[row], send_sem=send_a.at[step], recv_sem=recv_a.at[step],
            device_id={"row": to}, device_id_type=MESH)

    @pl.loop(1, rows)
    def _(step):
        scatter(step).start()

    @pl.loop(1, rows)
    def _(step):
        scatter(step).wait()

    summed = parts[0]
    for k in range(1, rows):
        summed = summed + parts[k]

    split = jnp.concatenate(pieces(summed), axis=0)

    def product(matrix):
        full = jnp.dot(split, matrix, preferred_element_type=F32)
        return full[0:16] + (full[16:32] + full[32:48])

    moved, left, across = product(move), product(prefix), product(whole)
    running = [jnp.zeros((1, BINS), F32)] * 2
    sides = [[], []]
    for which in range(2):
        for k in range(HIGH):
            at = which * HIGH + k
            sides[which].append(left[at:at + 1] + running[which])
            running[which] = running[which] + across[at:at + 1]
    grad_left, hess_left = (jnp.concatenate(side, axis=0) for side in sides)
    grad_all, hess_all = running
    grad_right = grad_all - grad_left
    gain = (grad_left * grad_left / (hess_left + 1.0)
            + grad_right * grad_right / (hess_all - hess_left + 1.0)
            - grad_all * grad_all / (hess_all + 1.0))
    shape = (HIGH, BINS)
    last = (iota(shape, 0) == HIGH - 1) & (iota(shape, 1) % LOW == LOW - 1)
    gain = jnp.where(last, -jnp.inf, gain)
    best = jnp.max(gain, axis=0, keepdims=True)
    for shift in (1, 2, 4, 8, 16):
        best = jnp.maximum(best, pltpu.roll(best, BINS - shift, 1))
    heads = iota((1, BINS), 1) % LOW == 0
    best = jnp.where(heads, best, -jnp.inf)
    top = jnp.max(best, axis=1, keepdims=True)
    tops[feat] = jnp.broadcast_to(top, (1, LANES))
    bests[row] = jnp.where(heads, best, 0.0)

    def spread_top(step):
        return pltpu.make_async_remote_copy(
            src_ref=tops.at[feat], dst_ref=tops.at[feat], send_sem=send_b.at[step], recv_sem=recv_b.at[step],
            device_id={"feat": lax.rem(feat + step, feats)}, device_id_type=MESH)

    @pl.loop(1, feats)
    def _(step):
        spread_top(step).start()

    block = iota(shape, 1) // LOW == iota(shape, 0)
    for which in range(2):
        whole_rows = moved[which * HIGH:(which + 1) * HIGH]
        placed = jnp.zeros(shape, F32)
        for shift in range(GROUP):
            turned = whole_rows if shift == 0 else pltpu.roll(whole_rows, shift * LOW, 1)
            turned = jnp.where(block, turned, 0.0)
            placed = placed + (turned if shift == 0 else pltpu.roll(turned, GROUP - shift, 0))
        blocks[row, :, which, :] = placed

    def to_rows(step, ref, send_sem, recv_sem):
        return pltpu.make_async_remote_copy(
            src_ref=ref.at[row], dst_ref=ref.at[row], send_sem=send_sem.at[step], recv_sem=recv_sem.at[step],
            device_id={"row": lax.rem(row + step, rows)}, device_id_type=MESH)

    @pl.loop(1, rows)
    def _(step):
        to_rows(step, blocks, send_c, recv_c).start()
        to_rows(step, bests, send_d, recv_d).start()

    @pl.loop(1, feats)
    def _(step):
        spread_top(step).wait()

    peaks[row] = jnp.max(tops[...], axis=0)

    @pl.loop(1, rows)
    def _(step):
        to_rows(step, peaks, send_e, recv_e).start()

    @pl.loop(1, rows)
    def _(step):
        to_rows(step, blocks, send_c, recv_c).wait()
        to_rows(step, bests, send_d, recv_d).wait()
    for k in range(rows):
        hist_ref[k * GROUP:(k + 1) * GROUP] = blocks[k]

    @pl.loop(1, rows)
    def _(step):
        to_rows(step, peaks, send_e, recv_e).wait()
    largest = jnp.max(jnp.max(peaks[...], axis=0), axis=1, keepdims=True)
    pick = as_bf16((source[:, :LANES] % LOW == 0) & (source[:, :LANES] // LOW == iota((BINS, LANES), 1) % GROUP))
    every = jnp.concatenate([bests[k] for k in range(rows)], axis=0)
    chosen = [jnp.dot(piece, pick, preferred_element_type=F32) for piece in pieces(every)]
    chosen = chosen[0] + (chosen[1] + chosen[2])
    mine = iota((rows, LANES), 1) // GROUP == iota((rows, LANES), 0)
    line = jnp.sum(jnp.where(mine, chosen, 0.0), axis=0, keepdims=True)
    gain_ref[...] = (line / (largest + 1e-6))[:, :rows * GROUP]


def gains_of(rows, feats, part):
    vmem = pl.BlockSpec(memory_space=pltpu.VMEM)
    groups = part.shape[0]
    dma = pltpu.SemaphoreType.DMA
    return pl.pallas_call(
        functools.partial(gain_kernel, rows, feats),
        out_shape=(jax.ShapeDtypeStruct((groups * GROUP, 2, BINS), F32), jax.ShapeDtypeStruct((1, groups * GROUP), F32)),
        in_specs=[vmem],
        out_specs=(vmem, vmem),
        scratch_shapes=[
            pltpu.VMEM((rows, 2 * HIGH, BINS), F32), pltpu.VMEM((rows, GROUP, 2, BINS), F32),
            pltpu.VMEM((rows, 1, BINS), F32), pltpu.VMEM((feats, 1, LANES), F32), pltpu.VMEM((rows, 1, LANES), F32),
            dma((rows,)), dma((rows,)), dma((feats,)), dma((feats,)), dma((rows,)), dma((rows,)),
            dma((rows,)), dma((rows,)), dma((rows,)), dma((rows,)),
        ],
        compiler_params=pltpu.CompilerParams(collective_id=1, has_side_effects=True, vmem_limit_bytes=32 * 2 ** 20),
        name="gains",
    )(part)


def shards(rows, feats, doc_scores, doc_labels, doc_ranks, query_tiles, bin_codes):
    tile_of = lambda x: x.reshape(8, LANES)
    gradient, hessian, lam = lambdas(feats, query_tiles, tile_of(doc_scores), tile_of(doc_labels), tile_of(doc_ranks))
    part = histograms(lam, bin_codes)
    histogram, split_gain = gains_of(rows, feats, part)
    return gradient.reshape(-1), hessian.reshape(-1), histogram, split_gain.reshape(-1)


def solution(mesh):
    return jax.shard_map(
        functools.partial(shards, mesh.shape["row"], mesh.shape["feat"]),
        mesh=mesh,
        in_specs=(P(("row", "feat")), P(("row", "feat")), P(("row", "feat")), P("row", None), P("feat", "row")),
        out_specs=(P(("row", "feat")), P(("row", "feat")), P("feat", None, None), P("feat")),
        check_vma=False,
    )
```

time: 1310 us -> 82.3 us (0.06); the launches traced: 1290 us -> 82.1 us
  matrix products: 517 us -> 0 us
  waiting for transfers between devices: 383 us -> 0 us
  blocking collectives: 163 us -> 0 us
  loops' own time: 103 us -> 0 us
  Pallas kernels: 0 us -> 73 us
  local copies, waits for them, and re-layouts: 62.6 us -> 8.44 us
  other arithmetic: 48.3 us -> 0 us
  between operations: 15.5 us -> 0.68 us
    dot_general x17 -> x0, matrix products: 517 us -> none  [the longest x16 514 us: add_block(): jnp.einsum('cr,frb->fcb', lambda_block, bin_hot, preferred_element_type=j...]
    psum x2 -> x0, waiting for transfers between devices: 383 us -> none  [the longest x1 321 us: shards(): summed = lax.psum(owned_lambdas, 'feat')]
    another operation x13 -> x0, loops' own time: 103 us -> none  [the longest x11 65.9 us: row_tile(): lax.fori_loop(0, tile_span[tile], col_tile, (empty_row, empty_row))]
    all_gather x3 -> x0, blocking collectives: 101 us -> none  [the longest x1 37.3 us: shards(): lax.all_gather(doc_scores, 'feat', axis=0, tiled=True)]
    pallas_call x0 -> x3, Pallas kernels: none -> 73 us  [the longest x1 26.6 us: histograms(): pl.pallas_call(functools.partial(histogram_kernel, groups, docs, unroll),...]
    pmax x1 -> x0, blocking collectives: 61.8 us -> none  [shards(): largest = lax.pmax(jnp.max(best), 'feat')]
    dynamic_slice x222 -> x0, local copies, waits for them, and re-layouts: 56.2 us -> none  [the longest x16 17.3 us: add_block(): lax.dynamic_slice_in_dim(bin_codes, block_index * block_rows, block_rows, 1)]
    reduce_sum x52 -> x0, other arithmetic: 38 us -> none  [the longest x43 32.6 us: pair_sums(): return (jnp.sum(terms, axis=1), jnp.sum(weight * rising * falling, axis=1))]
  transfers between devices with their start and end apart: 2 -> 0, of which waited for: 2 -> 0; matrix products, arithmetic and copies ran while one was open for 0% -> 0% of each run, Pallas kernels for 0% -> 0%
where the time goes in v1:
time: 82.3 us; the launch traced here: 82.1 us
  Pallas kernels  73 us (89%)
  local copies, waits for them, and re-layouts  8.44 us (10%)
    pallas_call x1, Pallas kernels, histograms(): pl.pallas_call(functools.partial(histogram_kernel, groups, docs, unroll),...  26.6 us
    pallas_call x1, Pallas kernels, lambdas(): pl.pallas_call(functools.partial(lambda_kernel, feats), out_shape=(block,...  24 us
    pallas_call x1, Pallas kernels, gains_of(): pl.pallas_call(functools.partial(gain_kernel, rows, feats), out_shape=(ja...  22.4 us
    unnamed x14, local copies, waits for them, and re-layouts  8.44 us

profile of v1, /device:TPU:1, one launch (start us, length us, event | category | flops | bytes accessed | tf_op | source)
XLA Modules:
  0.0 82.1 jit_solution(2190307096605702862)
XLA Ops:
  0.6 0.0 copy-start.1
  0.6 0.7 copy-done.1
  1.3 0.0 copy-start.2
  1.3 0.7 copy-done.2
  2.0 0.0 copy-start.3
  2.0 0.7 copy-done.3
  2.7 0.0 copy-start.4
  2.7 0.7 copy-done.4
  3.4 24.0 %lambdas.1 = (f32[8,128]{1,0:T(8,128)S(1)}, f32[8,128]{1,0:T(8,128)S(1)}, bf16[32,16,128]{2,1,0:T(8,128)(2,1)S(1)}) custom-call(s32[1,64]{1,0:T(1,128)S(1)} %copy-done.4, f32[8,128]{1,0:T(8,128)S(1)} %bitcast.6, s32[8,128]{1,0:T(8,128)S(1)} %bitcast.7, s32[8,128]{1,0:T(8,128)S(1)} %bitcast.8), custom_call_target="tpu_custom_call" | custom-call | tf_op jit(solution)/shard_map/lambdas/pallas_call | solution.py:162
  27.4 0.0 copy-start
  27.4 3.4 %copy-done = s32[64,32768]{1,0:T(8,128)S(1)} copy-done((s32[64,32768]{1,0:T(8,128)S(1)}, s32[64,32768]{1,0:T(8,128)}, u32[]{:S(2)}) %copy-start) | copy-done | bytes 8388632
  30.7 26.6 %histograms.1.part_ref = f32[8,16,256]{2,1,0:T(8,128)S(1)} custom-call(bf16[32,16,128]{2,1,0:T(8,128)(2,1)S(1)} %get-tuple-element.11.lam_ref, s32[64,32768]{1,0:T(8,128)S(1)} %copy-done), custom_call_target="tpu_custom_call" | custom-call | tf_op jit(solution)/shard_map/histograms/pallas_call | solution.py:243
  57.3 22.4 %gains.1 = (f32[64,2,256]{2,1,0:T(2,128)S(1)}, f32[1,64]{1,0:T(1,128)S(1)}) custom-call(f32[8,16,256]{2,1,0:T(8,128)S(1)} %histograms.1.part_ref), custom_call_target="tpu_custom_call" | custom-call | tf_op jit(solution)/shard_map/gains/pallas_call | solution.py:393
  79.7 0.6 copy.13
  80.3 0.6 copy.14
  80.9 0.7 copy.15
  81.6 0.5 copy.16
Async XLA Ops:
  0.6 0.7 copy-start.1
  1.3 0.7 copy-start.2
  2.0 0.7 copy-start.3
  2.7 0.7 copy-start.4
  27.4 3.4 %copy-start = (s32[64,32768]{1,0:T(8,128)S(1)}, s32[64,32768]{1,0:T(8,128)}, u32[]{:S(2)}) copy-start(s32[64,32768]{1,0:T(8,128)} %codes_ref.1) | copy-start | bytes 25165828

commit v2 on v1

v2 whole, which is shorter than its diff:
```python
import functools

import jax
import jax.experimental.pallas as pl
import jax.experimental.pallas.tpu as pltpu
import jax.numpy as jnp
from jax import lax
from jax.sharding import PartitionSpec as P

BINS = 256
MAX_TILES = 8
LANES = 128
QUERIES = 64
HIGH, LOW = 8, 32
GROUP = 8
MESH = pl.DeviceIdType.MESH
F32, BF16, F8, I8 = jnp.float32, jnp.bfloat16, jnp.float8_e4m3fn, jnp.int8


def iota(shape, dim):
    return lax.broadcasted_iota(jnp.int32, shape, dim)


def pieces(x):
    first = x.astype(BF16)
    rest = x - first.astype(F32)
    second = rest.astype(BF16)
    third = (rest - second.astype(F32)).astype(BF16)
    return first, second, third


def query_spans(tiles_ref, me):
    first = [jnp.int32(0)] * 8
    count = [jnp.int32(1)] * 8
    start = 8 - me * 8
    for query in range(QUERIES):
        tiles = tiles_ref[0, query]
        for tile in range(8):
            inside = start <= 8 + tile
            first[tile] = jnp.where(inside, start, first[tile])
            count[tile] = jnp.where(inside, tiles, count[tile])
        start = start + tiles
    return first, count


def discount_table():
    place = (iota((8, LANES), 0) * LANES + iota((8, LANES), 1)).astype(F32)
    return place, 1.0 / jnp.log2(place + 2.0)


def query_scale(window, first, count):
    place, table = discount_table()
    rows = iota((8, LANES), 0)
    first_rows, count_rows = jnp.zeros((8, LANES), jnp.int32), jnp.zeros((8, LANES), jnp.int32)
    for tile in range(8):
        first_rows = jnp.where(rows == tile, first[tile], first_rows)
        count_rows = jnp.where(rows == tile, count[tile], count_rows)
    all_gains = window[1]
    reach = jnp.concatenate([(all_gains >= F32(2 ** level - 1)).astype(F32) for level in range(1, 5)], axis=0)
    reach = jnp.broadcast_to(jnp.sum(reach, axis=1, keepdims=True), (96, LANES))
    above = [jnp.zeros((8, LANES), F32)] * 4
    for tile in range(24):
        member = (first_rows <= tile) & (first_rows + count_rows > tile)
        for level in range(4):
            at = level * 24 + tile
            above[level] = above[level] + jnp.where(member, jnp.broadcast_to(reach[at:at + 1], (8, LANES)), 0.0)
    ideals = []
    for tile in range(8):
        total = jnp.zeros((8, LANES), F32)
        for level in range(4):
            limit = jnp.broadcast_to(above[level][tile:tile + 1], (8, LANES))
            total = total + jnp.where(place < limit, table * F32(2 ** level), 0.0)
        ideals.append(jnp.sum(total, axis=0, keepdims=True))
    ideal = jnp.sum(jnp.concatenate(ideals, axis=0), axis=1, keepdims=True)
    return 1.0 / (1.0 + ideal)


def widen(window, wide, slot):
    for which in range(3):
        turned = jnp.transpose(window[which, slot * 8:slot * 8 + 8, :])
        for tile in range(8):
            wide[which, slot * 8 + tile] = jnp.broadcast_to(turned[:, tile:tile + 1], (LANES, LANES))


def pair_sums(own, wide, first, count):
    odds, gains, discs = own
    grads, hessians = [], []
    rows = 32
    for tile in range(8):
        odds_i, gain_i, disc_i = (jnp.broadcast_to(x[tile:tile + 1], (rows, LANES)) for x in own)

        def column(step, carried):
            at = jnp.minimum(jnp.maximum(first[tile] + step, 0), 23)
            valid = jnp.where(step < count[tile], F32(1), F32(0))
            grad, hess = carried
            for part in range(0, LANES, rows):
                odds_j, gain_j, disc_j = (wide[which, at, part:part + rows, :] for which in range(3))
                inverse = pl.reciprocal(odds_i + odds_j, approx=True)
                delta = gain_i - gain_j
                weight = delta * (jnp.abs(disc_i - disc_j) * (inverse * valid))
                grad = grad + weight * jnp.where(delta > 0, odds_j, odds_i)
                hess = hess + jnp.abs(weight) * (inverse * odds_j)
            return grad, hess

        empty = jnp.zeros((rows, LANES), F32)
        grad, hess = lax.fori_loop(0, MAX_TILES, column, (empty, empty))
        grads.append(jnp.sum(grad, axis=0, keepdims=True))
        hessians.append(jnp.sum(hess, axis=0, keepdims=True))
    return jnp.concatenate(grads, axis=0), jnp.concatenate(hessians, axis=0)


def build_matrices(matrices):
    source, target = iota((BINS, BINS), 0), iota((BINS, BINS), 1)
    source_low, source_feat = source >> 3, source & 7
    target_feat, target_low = target >> 5, target & 31
    same = source_feat == target_feat
    for k, flag in enumerate((same & (source_low == target_low), same & (source_low <= target_low), same)):
        matrices[k] = jnp.where(flag, F32(1), F32(0)).astype(BF16)
    pick = ((source & (LOW - 1)) == 0) & ((source >> 5) == (target & 7))
    matrices[3] = jnp.where(pick, F32(1), F32(0)).astype(BF16)


def round_kernel(rows, ys, zs, *refs):
    accumulators = ([pltpu.ACC(k % 2)((2 * HIGH * GROUP, BINS), F32) for k in range(rows)]
                    + [pltpu.ACC(k % 2)((48, BINS), F32) for k in range(3)] + [pltpu.ACC(0)((32, BINS), F32)])
    pl.run_scoped(lambda *accs: round_body(rows, ys, zs, accs[:rows], accs[rows:], *refs), *accumulators)


def round_body(rows, ys, zs, accs, small, tiles_hbm, score_hbm, label_hbm, rank_hbm, codes_hbm,
                 grad_ref, hess_ref, hist_ref, gain_ref,
                 tiles_ref, score_ref, label_ref, rank_ref, codes,
                 window, wide, gathered, spread, matrices, mine, parts, blocks, bests, tops_z, tops_y,
                 in_sem, code_sem, halo_send, halo_recv, send_z, recv_z, send_y, recv_y,
                 send_a, recv_a, send_b, recv_b, send_c, recv_c, send_d, recv_d, send_e, recv_e):
    row, feat = lax.axis_index("row"), lax.axis_index("feat")
    feats = ys * zs
    y, z = feat // zs, lax.rem(feat, zs)
    groups = codes.shape[0] // GROUP
    chunks = codes.shape[1] // 1024

    loads = [pltpu.make_async_copy(src, dst, in_sem.at[k]) for k, (src, dst) in enumerate(
        ((score_hbm, score_ref), (label_hbm, label_ref), (rank_hbm, rank_ref), (tiles_hbm, tiles_ref)))]
    for load in loads:
        load.start()
    code_loads = [pltpu.make_async_copy(codes_hbm.at[pl.ds(k * GROUP, GROUP), :], codes.at[pl.ds(k * GROUP, GROUP), :],
                                        code_sem.at[k]) for k in range(groups)]

    barrier = pltpu.get_barrier_semaphore()

    def at_row(step):
        return {"row": lax.rem(row + step, rows)}

    def at_z(step):
        return {"feat": y * zs + lax.rem(z + step, zs)}

    def at_y(step):
        return {"feat": lax.rem(y + step, ys) * zs + z}

    def at_feat(step):
        return {"feat": lax.rem(feat + step, feats)}

    def signal(device):
        pl.semaphore_signal(barrier, inc=1, device_id=device, device_id_type=MESH)

    signal(at_feat(1))
    signal(at_feat(feats - 1))
    for step in range(1, zs):
        signal(at_z(step))
    for step in range(1, ys):
        signal(at_y(step))
    for step in range(1, rows):
        signal(at_row(step))
    for load in loads:
        load.wait()
    for load in code_loads:
        load.start()

    odds = jnp.exp(score_ref[...])
    gains = (jnp.left_shift(1, label_ref[...]) - 1).astype(F32)
    discs = 1.0 / jnp.log2(rank_ref[...].astype(F32) + 2.0)
    own = (odds, gains, discs)
    for which in range(3):
        window[which, 8:16, :] = own[which]
    build_matrices(matrices)
    pl.semaphore_wait(barrier, 2 + zs - 1 + ys - 1 + rows - 1)
    halos = []
    for side, (target, place) in enumerate(((feats - 1, 16), (1, 0))):
        copy = pltpu.make_async_remote_copy(
            src_ref=window.at[:, pl.ds(8, 8), :], dst_ref=window.at[:, pl.ds(place, 8), :],
            send_sem=halo_send.at[side], recv_sem=halo_recv.at[side],
            device_id=at_feat(target), device_id_type=MESH)
        copy.start()
        halos.append(copy)
    first, count = query_spans(tiles_ref, feat)
    widen(window, wide, 1)
    for copy in halos:
        copy.wait()
    widen(window, wide, 0)
    widen(window, wide, 2)
    scale = query_scale(window, first, count)
    grad, hess = pair_sums(own, wide, first, count)
    grad = -grad * scale
    hess = hess * (odds * scale)
    grad_ref[...] = grad
    hess_ref[...] = hess
    gathered[feat] = jnp.concatenate([grad, hess], axis=0).astype(BF16)

    def over_z(step):
        return pltpu.make_async_remote_copy(
            src_ref=gathered.at[feat], dst_ref=gathered.at[feat], send_sem=send_z.at[step], recv_sem=recv_z.at[step],
            device_id=at_z(step), device_id_type=MESH)

    def over_y(step):
        block = gathered.at[pl.ds(y * zs, zs)]
        return pltpu.make_async_remote_copy(
            src_ref=block, dst_ref=block, send_sem=send_y.at[step], recv_sem=recv_y.at[step],
            device_id=at_y(step), device_id_type=MESH)

    for step in range(1, zs):
        over_z(step).start()
    for load in code_loads:
        load.wait()

    def scatter(group):
        return pltpu.make_async_remote_copy(
            src_ref=mine.at[group], dst_ref=parts.at[row], send_sem=send_a.at[group], recv_sem=recv_a.at[row],
            device_id={"row": jnp.int32(group)}, device_id_type=MESH)

    def arrival(step):
        source = lax.rem(row + step, rows)
        return pltpu.make_async_remote_copy(
            src_ref=parts.at[source], dst_ref=parts.at[source], send_sem=send_a.at[source], recv_sem=recv_a.at[source],
            device_id=at_row(step), device_id_type=MESH)

    zero = jnp.zeros((), BF16)

    @pl.loop(0, chunks)
    def _(turn):
        @pl.when(turn == 1)
        def _():
            for step in range(1, zs):
                over_z(step).wait()
            for step in range(1, ys):
                over_y(step).start()

        for step in range(1, ys):
            @pl.when(turn == step * zs)
            def _():
                over_y(ys - step).wait()

        owner = lax.rem(y + turn // zs, ys) * zs + lax.rem(z + lax.rem(turn, zs), zs)
        part = gathered[owner].astype(F32)
        for which in range(2):
            for tile in range(8):
                line = which * 8 + tile
                spread[which, :, tile * LANES:(tile + 1) * LANES] = jnp.broadcast_to(
                    part[line:line + 1], (16, LANES)).astype(BF16)
        for k in range(1024 // BINS):
            at = pl.ds(pl.multiple_of(owner * 1024 + k * BINS, BINS), BINS)
            lam = [spread[which, :, k * BINS:(k + 1) * BINS] for which in range(2)]
            for group in range(groups):
                code = codes[group * GROUP:(group + 1) * GROUP, at]
                high = (code >> 5).astype(F32)
                high = jnp.concatenate([high, high - 1.0], axis=0).astype(BF16)
                hits = [high == jnp.array(2 * k, BF16) for k in range(HIGH // 2)]
                lhs = jnp.concatenate([jnp.where(hit, value, zero) for value in lam for hit in hits], axis=0)
                low = code & (LOW - 1)
                low = jnp.concatenate([low - k for k in range(4)], axis=0).astype(I8)
                rhs = jnp.concatenate(
                    [jnp.where(low == jnp.array(4 * k, I8), jnp.ones((), F8), jnp.zeros((), F8))
                     for k in range(LOW // 4)], axis=0)
                stage = group // 2 % 2
                pltpu.matmul_push_rhs(rhs, stage, group % 2, transpose=True)
                pltpu.matmul_acc_lhs(accs[group], lhs, load_staged_rhs=stage)

    shape = (2 * HIGH, GROUP, BINS)
    same = iota(shape, 1) == (iota(shape, 2) & (GROUP - 1))
    for group in range(groups):
        total = pltpu.matmul_pop(accs[group]).reshape(shape)
        mine[group] = jnp.sum(jnp.where(same, total, 0.0), axis=1)

        @pl.when(row != group)
        def _():
            scatter(group).start()


    parts[row] = mine[row]
    for step in range(1, rows):
        arrival(step).wait_recv()
    summed = parts[0]
    for k in range(1, rows):
        summed = summed + parts[k]

    split = jnp.concatenate(pieces(summed), axis=0)
    for k in range(3):
        pltpu.matmul_push_rhs(matrices[k], k // 2, k % 2)
        pltpu.matmul_acc_lhs(small[k], split, load_staged_rhs=k // 2)

    def product(k):
        full = pltpu.matmul_pop(small[k])
        return full[0:16] + (full[16:32] + full[32:48])

    left, across, moved = product(1), product(2), product(0)
    running = [jnp.zeros((1, BINS), F32)] * 2
    sides = [[], []]
    for which in range(2):
        for k in range(HIGH):
            at = which * HIGH + k
            sides[which].append(left[at:at + 1] + running[which])
            running[which] = running[which] + across[at:at + 1]
    grad_left, hess_left = (jnp.concatenate(side, axis=0) for side in sides)
    grad_all, hess_all = running
    grad_right = grad_all - grad_left
    gain = (grad_left * grad_left / (hess_left + 1.0)
            + grad_right * grad_right / (hess_all - hess_left + 1.0)
            - grad_all * grad_all / (hess_all + 1.0))
    shape = (HIGH, BINS)
    last = (iota(shape, 0) == HIGH - 1) & ((iota(shape, 1) & (LOW - 1)) == LOW - 1)
    gain = jnp.where(last, -jnp.inf, gain)
    best = jnp.max(gain, axis=0, keepdims=True)
    for shift in (1, 2, 4, 8, 16):
        best = jnp.maximum(best, pltpu.roll(best, BINS - shift, 1))
    heads = (iota((1, BINS), 1) & (LOW - 1)) == 0
    bests[row] = jnp.where(heads, best, 0.0)

    def to_rows(step, ref, send_sem, recv_sem):
        return pltpu.make_async_remote_copy(
            src_ref=ref.at[row], dst_ref=ref.at[row], send_sem=send_sem.at[step], recv_sem=recv_sem.at[step],
            device_id=at_row(step), device_id_type=MESH)

    for step in range(1, rows):
        to_rows(step, bests, send_b, recv_b).start()

    block = (iota(shape, 1) >> 5) == iota(shape, 0)
    for which in range(2):
        whole_rows = moved[which * HIGH:(which + 1) * HIGH]
        placed = jnp.zeros(shape, F32)
        for shift in range(GROUP):
            turned = whole_rows if shift == 0 else pltpu.roll(whole_rows, shift * LOW, 1)
            turned = jnp.where(block, turned, 0.0)
            placed = placed + (turned if shift == 0 else pltpu.roll(turned, GROUP - shift, 0))
        blocks[row, :, which, :] = placed

    for step in range(1, rows):
        to_rows(step, bests, send_b, recv_b).wait()
    every = jnp.concatenate([bests[k] for k in range(rows)], axis=0)
    here = (iota((rows, BINS), 1) & (LOW - 1)) == 0
    top = jnp.max(jnp.where(here, every, -jnp.inf), axis=0, keepdims=True)
    tops_z[z] = jnp.broadcast_to(jnp.max(top, axis=1, keepdims=True), (1, LANES))

    def top_z(step):
        return pltpu.make_async_remote_copy(
            src_ref=tops_z.at[z], dst_ref=tops_z.at[z], send_sem=send_c.at[step], recv_sem=recv_c.at[step],
            device_id=at_z(step), device_id_type=MESH)

    def top_y(step):
        return pltpu.make_async_remote_copy(
            src_ref=tops_y.at[y], dst_ref=tops_y.at[y], send_sem=send_d.at[step], recv_sem=recv_d.at[step],
            device_id=at_y(step), device_id_type=MESH)

    for step in range(1, zs):
        top_z(step).start()
    for step in range(1, rows):
        to_rows(step, blocks, send_e, recv_e).start()
    split = jnp.concatenate([piece.astype(F32) for piece in pieces(every)] + [jnp.zeros((rows, BINS), F32)], axis=0)
    pltpu.matmul_push_rhs(matrices[3], 0, 0)
    pltpu.matmul_acc_lhs(small[3], split.astype(BF16), load_staged_rhs=0)
    full = pltpu.matmul_pop(small[3])
    chosen = full[0:rows] + (full[rows:2 * rows] + full[2 * rows:3 * rows])
    owned = (iota((rows, BINS), 1) >> 3) == iota((rows, BINS), 0)
    line = jnp.sum(jnp.where(owned, chosen, 0.0), axis=0, keepdims=True)
    for step in range(1, zs):
        top_z(step).wait()
    tops_y[y] = jnp.max(tops_z[...], axis=0)
    for step in range(1, ys):
        top_y(step).start()
    for step in range(1, rows):
        to_rows(step, blocks, send_e, recv_e).wait()
    for k in range(rows):
        hist_ref[k * GROUP:(k + 1) * GROUP] = blocks[k]
    for group in range(groups):
        @pl.when(row != group)
        def _():
            scatter(group).wait_send()
    for step in range(1, ys):
        top_y(step).wait()
    largest = jnp.max(tops_y[...], axis=0)
    gain_ref[...] = (line[:, :LANES] / (largest + 1e-6))[:, :rows * GROUP]


def one_round(rows, ys, zs, tiles, scores, labels, ranks, codes):
    vmem = pl.BlockSpec(memory_space=pltpu.VMEM)
    hbm = pl.BlockSpec(memory_space=pltpu.HBM)
    here, docs = codes.shape
    groups = here // GROUP
    feats = ys * zs
    block = pltpu.VMEM((8, LANES), F32)
    dma = pltpu.SemaphoreType.DMA
    pair = lambda n: [dma((n,)), dma((n,))]
    return pl.pallas_call(
        functools.partial(round_kernel, rows, ys, zs),
        out_shape=(block, block, pltpu.VMEM((here, 2, BINS), F32), pltpu.VMEM((1, here), F32)),
        in_specs=[hbm] * 5,
        out_specs=(vmem,) * 4,
        scratch_shapes=[
            pltpu.SMEM((1, QUERIES), jnp.int32), pltpu.VMEM((8, LANES), F32), pltpu.VMEM((8, LANES), jnp.int32),
            pltpu.VMEM((8, LANES), jnp.int32), pltpu.VMEM((here, docs), jnp.int32),
            pltpu.VMEM((3, 24, LANES), F32), pltpu.VMEM((3, 24, LANES, LANES), F32), pltpu.VMEM((feats, 16, LANES), BF16),
            pltpu.VMEM((2, 16, 1024), BF16), pltpu.VMEM((4, BINS, BINS), BF16),
            pltpu.VMEM((groups, 2 * HIGH, BINS), F32), pltpu.VMEM((rows, 2 * HIGH, BINS), F32),
            pltpu.VMEM((rows, GROUP, 2, BINS), F32), pltpu.VMEM((rows, 1, BINS), F32),
            pltpu.VMEM((zs, 1, LANES), F32), pltpu.VMEM((ys, 1, LANES), F32),
            dma((4,)), dma((groups,)), *pair(2), *pair(zs), *pair(ys),
            *pair(rows), *pair(rows), *pair(zs), *pair(ys), *pair(rows),
        ],
        compiler_params=pltpu.CompilerParams(collective_id=0, has_side_effects=True, vmem_limit_bytes=60 * 2 ** 20),
        name="round",
    )(tiles, scores, labels, ranks, codes)


def publish_kernel(*refs):
    sems = refs[-1]
    half = (len(refs) - 1) // 2
    copies = [pltpu.make_async_copy(refs[k], refs[half + k], sems.at[k]) for k in range(half)]
    for copy in copies:
        copy.start()
    for copy in copies:
        copy.wait()


def publish(arrays):
    hbm = pl.BlockSpec(memory_space=pltpu.HBM)
    return pl.pallas_call(
        publish_kernel,
        out_shape=tuple(jax.ShapeDtypeStruct(x.shape, x.dtype) for x in arrays),
        in_specs=[pl.BlockSpec(memory_space=pltpu.VMEM)] * len(arrays),
        out_specs=(hbm,) * len(arrays),
        scratch_shapes=[pltpu.SemaphoreType.DMA((len(arrays),))],
        name="publish",
    )(*[pltpu.with_memory_space_constraint(x, pltpu.VMEM) for x in arrays])


def shards(rows, ys, zs, doc_scores, doc_labels, doc_ranks, query_tiles, bin_codes):
    tile_of = lambda x: x.reshape(8, LANES)
    gradient, hessian, histogram, split_gain = one_round(
        rows, ys, zs, query_tiles, tile_of(doc_scores), tile_of(doc_labels), tile_of(doc_ranks), bin_codes)
    gradient, hessian, histogram, split_gain = publish((gradient, hessian, histogram, split_gain))
    return gradient.reshape(-1), hessian.reshape(-1), histogram, split_gain.reshape(-1)


def solution(mesh):
    return jax.shard_map(
        functools.partial(shards, mesh.shape["row"], 4, mesh.shape["feat"] // 4),
        mesh=mesh,
        in_specs=(P(("row", "feat")), P(("row", "feat")), P(("row", "feat")), P("row", None), P("feat", "row")),
        out_specs=(P(("row", "feat")), P(("row", "feat")), P("feat", None, None), P("feat")),
        check_vma=False,
    )
```

time: 82.3 us -> 59.6 us (0.72)
  Pallas kernels: 73 us -> 58.8 us
  local copies, waits for them, and re-layouts: 8.44 us -> 0 us
    pallas_call x3 -> x2, Pallas kernels: 73 us -> 58.8 us  [the longest x1 58.1 us: one_round(): pl.pallas_call(functools.partial(round_kernel, rows, ys, zs), out_shape=(...]
    unnamed x14 -> x0, local copies, waits for them, and re-layouts: 8.44 us -> none
where the time goes in v2:
time: 59.6 us; the launch traced here: 59.5 us
  Pallas kernels  58.8 us (99%)
  between operations  0.64 us (1%)
    pallas_call x1, Pallas kernels, one_round(): pl.pallas_call(functools.partial(round_kernel, rows, ys, zs), out_shape=(...  58.1 us

profile of v2, /device:TPU:1, one launch (start us, length us, event | category | flops | bytes accessed | tf_op | source)
XLA Modules:
  0.0 59.5 jit_solution(11311420343001672908)
XLA Ops:
  0.6 58.1 %round.1 = (f32[8,128]{1,0:T(8,128)S(1)}, f32[8,128]{1,0:T(8,128)S(1)}, f32[64,2,256]{2,1,0:T(2,128)S(1)}, f32[1,64]{1,0:T(1,128)S(1)}) custom-call(s32[1,64]{1,0:T(1,128)} %refs_0_.1, f32[8,128]{1,0:T(8,128)} %bitcast.6, s32[8,128]{1,0:T(8,128)} %bitcast.7, s32[8,128]{1,0:T(8,128)} %bitcast.8, s32[64,32768]{1,0:T(8,128)} %refs_4_.1), custom_call_target="tpu_custom_call" | custom-call | tf_op jit(solution)/shard_map/round/pallas_call | solution.py:400
  58.8 0.7 %publish.1 = (f32[8,128]{1,0:T(8,128)}, f32[8,128]{1,0:T(8,128)}, f32[64,2,256]{2,1,0:T(2,128)}, f32[1,64]{1,0:T(1,128)}) custom-call(f32[8,128]{1,0:T(8,128)S(1)} %get-tuple-element.12.refs_0_, f32[8,128]{1,0:T(8,128)S(1)} %get-tuple-element.13.refs_1_, f32[64,2,256]{2,1,0:T(2,128)S(1)} %get-tuple-element.14.refs_2_, f32[1,64]{1,0:T(1,128)S(1)} %get-tuple-element.15.refs_3_), custom_call_target="tpu_custom_call" | custom-call | tf_op jit(solution)/shard_map/publish/pallas_call | solution.py:433

commit v3 on v2

--- a/solution.py
+++ b/solution.py
@@ -90,14 +90,13 @@
         odds_i, gain_i, disc_i = (jnp.broadcast_to(x[tile:tile + 1], (rows, LANES)) for x in own)
 
         def column(step, carried):
-            at = jnp.minimum(jnp.maximum(first[tile] + step, 0), 23)
-            valid = jnp.where(step < count[tile], F32(1), F32(0))
+            at = jnp.where(step < count[tile], jnp.minimum(jnp.maximum(first[tile] + step, 0), 23), 24)
             grad, hess = carried
             for part in range(0, LANES, rows):
                 odds_j, gain_j, disc_j = (wide[which, at, part:part + rows, :] for which in range(3))
                 inverse = pl.reciprocal(odds_i + odds_j, approx=True)
                 delta = gain_i - gain_j
-                weight = delta * (jnp.abs(disc_i - disc_j) * (inverse * valid))
+                weight = delta * (jnp.abs(disc_i - disc_j) * inverse)
                 grad = grad + weight * jnp.where(delta > 0, odds_j, odds_i)
                 hess = hess + jnp.abs(weight) * (inverse * odds_j)
             return grad, hess
@@ -129,9 +128,9 @@
 def round_body(rows, ys, zs, accs, small, tiles_hbm, score_hbm, label_hbm, rank_hbm, codes_hbm,
                  grad_ref, hess_ref, hist_ref, gain_ref,
                  tiles_ref, score_ref, label_ref, rank_ref, codes,
-                 window, wide, gathered, spread, matrices, mine, parts, blocks, bests, tops_z, tops_y,
+                 window, wide, gathered, spread, matrices, mine, parts, blocks, bests, tops,
                  in_sem, code_sem, halo_send, halo_recv, send_z, recv_z, send_y, recv_y,
-                 send_a, recv_a, send_b, recv_b, send_c, recv_c, send_d, recv_d, send_e, recv_e):
+                 send_a, recv_a, send_b, recv_b, send_c, recv_c, send_e, recv_e):
     row, feat = lax.axis_index("row"), lax.axis_index("feat")
     feats = ys * zs
     y, z = feat // zs, lax.rem(feat, zs)
@@ -142,8 +141,15 @@
         ((score_hbm, score_ref), (label_hbm, label_ref), (rank_hbm, rank_ref), (tiles_hbm, tiles_ref)))]
     for load in loads:
         load.start()
-    code_loads = [pltpu.make_async_copy(codes_hbm.at[pl.ds(k * GROUP, GROUP), :], codes.at[pl.ds(k * GROUP, GROUP), :],
-                                        code_sem.at[k]) for k in range(groups)]
+    y_low, y_high = lax.rem(y, 2), y // 2
+
+    def y_block(step):
+        return lax.rem(y_high + step // 2, 2) * 2 + lax.rem(y_low + step % 2, 2)
+
+    def code_load(step):
+        docs = pl.ds(pl.multiple_of(y_block(step) * (zs * 1024), zs * 1024), zs * 1024)
+        return pltpu.make_async_copy(codes_hbm.at[:, docs], codes.at[:, docs], code_sem.at[step])
+
 
     barrier = pltpu.get_barrier_semaphore()
 
@@ -154,7 +160,13 @@
         return {"feat": y * zs + lax.rem(z + step, zs)}
 
     def at_y(step):
-        return {"feat": lax.rem(y + step, ys) * zs + z}
+        return {"feat": y_block(step) * zs + z}
+
+    def at_row_y(step):
+        return {"row": lax.rem(row + step // 2, rows), "feat": y_block(step % 2) * zs + z}
+
+    def at_z_y(step):
+        return {"feat": y_block(step % 2 * 2) * zs + lax.rem(z + step // 2, zs)}
 
     def at_feat(step):
         return {"feat": lax.rem(feat + step, feats)}
@@ -164,16 +176,13 @@
 
     signal(at_feat(1))
     signal(at_feat(feats - 1))
-    for step in range(1, zs):
-        signal(at_z(step))
-    for step in range(1, ys):
-        signal(at_y(step))
-    for step in range(1, rows):
-        signal(at_row(step))
+    for step in range(1, 2 * zs):
+        signal(at_z_y(step))
+    signal(at_y(3))
+    for step in range(1, 2 * rows):
+        signal(at_row_y(step))
     for load in loads:
         load.wait()
-    for load in code_loads:
-        load.start()
 
     odds = jnp.exp(score_ref[...])
     gains = (jnp.left_shift(1, label_ref[...]) - 1).astype(F32)
@@ -181,8 +190,10 @@
     own = (odds, gains, discs)
     for which in range(3):
         window[which, 8:16, :] = own[which]
+    for which, value in enumerate((0.0, -1.0, 0.0)):
+        wide[which, 24] = jnp.full((LANES, LANES), value, F32)
     build_matrices(matrices)
-    pl.semaphore_wait(barrier, 2 + zs - 1 + ys - 1 + rows - 1)
+    pl.semaphore_wait(barrier, 2 + 2 * zs - 1 + 1 + 2 * rows - 1)
     halos = []
     for side, (target, place) in enumerate(((feats - 1, 16), (1, 0))):
         copy = pltpu.make_async_remote_copy(
@@ -191,10 +202,13 @@
             device_id=at_feat(target), device_id_type=MESH)
         copy.start()
         halos.append(copy)
+    code_load(0).start()
     first, count = query_spans(tiles_ref, feat)
     widen(window, wide, 1)
     for copy in halos:
         copy.wait()
+    for step in range(1, ys):
+        code_load(step).start()
     widen(window, wide, 0)
     widen(window, wide, 2)
     scale = query_scale(window, first, count)
@@ -216,10 +230,10 @@
             src_ref=block, dst_ref=block, send_sem=send_y.at[step], recv_sem=recv_y.at[step],
             device_id=at_y(step), device_id_type=MESH)
 
-    for step in range(1, zs):
+    offsets = [(turn + 1) // 2 if turn % 2 else zs - turn // 2 for turn in range(1, zs)]
+    for step in offsets:
         over_z(step).start()
-    for load in code_loads:
-        load.wait()
+    code_load(0).wait()
 
     def scatter(group):
         return pltpu.make_async_remote_copy(
@@ -236,19 +250,27 @@
 
     @pl.loop(0, chunks)
     def _(turn):
-        @pl.when(turn == 1)
-        def _():
-            for step in range(1, zs):
-                over_z(step).wait()
-            for step in range(1, ys):
-                over_y(step).start()
+        for at in range(1, 5):
+            @pl.when(turn == at)
+            def _():
+                for offset in offsets[at - 1:at] if at < 4 else offsets[at - 1:]:
+                    over_z(zs - offset).wait_recv()
+                if at == 4:
+                    for step in range(1, ys):
+                        over_y(step).start()
 
         for step in range(1, ys):
             @pl.when(turn == step * zs)
             def _():
-                over_y(ys - step).wait()
-
-        owner = lax.rem(y + turn // zs, ys) * zs + lax.rem(z + lax.rem(turn, zs), zs)
+                over_y(step).wait_recv()
+                code_load(step).wait()
+
+        inner = lax.rem(turn, zs)
+        odd = lax.rem(inner, 2)
+        offset = odd * ((inner + 1) // 2) + (1 - odd) * (zs - inner // 2)
+        outer = turn // zs
+        owner_y = lax.rem(y_high + outer // 2, 2) * 2 + lax.rem(y_low + lax.rem(outer, 2), 2)
+        owner = owner_y * zs + lax.rem(z + offset, zs)
         part = gathered[owner].astype(F32)
         for which in range(2):
             for tile in range(8):
@@ -284,6 +306,10 @@
             scatter(group).start()
 
 
+    for step in range(1, zs):
+        over_z(step).wait_send()
+    for step in range(1, ys):
+        over_y(step).wait_send()
     parts[row] = mine[row]
     for step in range(1, rows):
         arrival(step).wait_recv()
@@ -317,19 +343,21 @@
     shape = (HIGH, BINS)
     last = (iota(shape, 0) == HIGH - 1) & ((iota(shape, 1) & (LOW - 1)) == LOW - 1)
     gain = jnp.where(last, -jnp.inf, gain)
-    best = jnp.max(gain, axis=0, keepdims=True)
-    for shift in (1, 2, 4, 8, 16):
-        best = jnp.maximum(best, pltpu.roll(best, BINS - shift, 1))
-    heads = (iota((1, BINS), 1) & (LOW - 1)) == 0
-    bests[row] = jnp.where(heads, best, 0.0)
-
-    def to_rows(step, ref, send_sem, recv_sem):
-        return pltpu.make_async_remote_copy(
-            src_ref=ref.at[row], dst_ref=ref.at[row], send_sem=send_sem.at[step], recv_sem=recv_sem.at[step],
+    place_a = row * 2 + y_low
+    bests[place_a] = jnp.max(gain, axis=0, keepdims=True)
+
+    def send_best(step):
+        return pltpu.make_async_remote_copy(
+            src_ref=bests.at[place_a], dst_ref=bests.at[place_a], send_sem=send_b.at[step], recv_sem=recv_b.at[step],
+            device_id=at_row_y(step), device_id_type=MESH)
+
+    for step in range(1, 2 * rows):
+        send_best(step).start()
+
+    def send_block(step):
+        return pltpu.make_async_remote_copy(
+            src_ref=blocks.at[row], dst_ref=blocks.at[row], send_sem=send_e.at[step], recv_sem=recv_e.at[step],
             device_id=at_row(step), device_id_type=MESH)
-
-    for step in range(1, rows):
-        to_rows(step, bests, send_b, recv_b).start()
 
     block = (iota(shape, 1) >> 5) == iota(shape, 0)
     for which in range(2):
@@ -341,27 +369,25 @@
             placed = placed + (turned if shift == 0 else pltpu.roll(turned, GROUP - shift, 0))
         blocks[row, :, which, :] = placed
 
+    for step in range(1, 2 * rows):
+        send_best(step).wait()
+    top = jnp.max(bests[...], axis=0)
+    place_b = z * 2 + y_high
+    tops[place_b] = jnp.broadcast_to(jnp.max(top, axis=1, keepdims=True), (1, LANES))
+
+    def send_top(step):
+        return pltpu.make_async_remote_copy(
+            src_ref=tops.at[place_b], dst_ref=tops.at[place_b], send_sem=send_c.at[step], recv_sem=recv_c.at[step],
+            device_id=at_z_y(step), device_id_type=MESH)
+
+    for step in range(1, 2 * zs):
+        send_top(step).start()
     for step in range(1, rows):
-        to_rows(step, bests, send_b, recv_b).wait()
-    every = jnp.concatenate([bests[k] for k in range(rows)], axis=0)
-    here = (iota((rows, BINS), 1) & (LOW - 1)) == 0
-    top = jnp.max(jnp.where(here, every, -jnp.inf), axis=0, keepdims=True)
-    tops_z[z] = jnp.broadcast_to(jnp.max(top, axis=1, keepdims=True), (1, LANES))
-
-    def top_z(step):
-        return pltpu.make_async_remote_copy(
-            src_ref=tops_z.at[z], dst_ref=tops_z.at[z], send_sem=send_c.at[step], recv_sem=recv_c.at[step],
-            device_id=at_z(step), device_id_type=MESH)
-
-    def top_y(step):
-        return pltpu.make_async_remote_copy(
-            src_ref=tops_y.at[y], dst_ref=tops_y.at[y], send_sem=send_d.at[step], recv_sem=recv_d.at[step],
-            device_id=at_y(step), device_id_type=MESH)
-
-    for step in range(1, zs):
-        top_z(step).start()
-    for step in range(1, rows):
-        to_rows(step, blocks, send_e, recv_e).start()
+        send_block(step).start()
+    every = jnp.concatenate([bests[k * 2 + y_low] for k in range(rows)], axis=0)
+    for shift in (1, 2, 4, 8, 16):
+        every = jnp.maximum(every, pltpu.roll(every, BINS - shift, 1))
+    every = jnp.where((iota((rows, BINS), 1) & (LOW - 1)) == 0, every, 0.0)
     split = jnp.concatenate([piece.astype(F32) for piece in pieces(every)] + [jnp.zeros((rows, BINS), F32)], axis=0)
     pltpu.matmul_push_rhs(matrices[3], 0, 0)
     pltpu.matmul_acc_lhs(small[3], split.astype(BF16), load_staged_rhs=0)
@@ -369,22 +395,17 @@
     chosen = full[0:rows] + (full[rows:2 * rows] + full[2 * rows:3 * rows])
     owned = (iota((rows, BINS), 1) >> 3) == iota((rows, BINS), 0)
     line = jnp.sum(jnp.where(owned, chosen, 0.0), axis=0, keepdims=True)
-    for step in range(1, zs):
-        top_z(step).wait()
-    tops_y[y] = jnp.max(tops_z[...], axis=0)
-    for step in range(1, ys):
-        top_y(step).start()
     for step in range(1, rows):
-        to_rows(step, blocks, send_e, recv_e).wait()
+        send_block(step).wait()
     for k in range(rows):
         hist_ref[k * GROUP:(k + 1) * GROUP] = blocks[k]
     for group in range(groups):
         @pl.when(row != group)
         def _():
             scatter(group).wait_send()
-    for step in range(1, ys):
-        top_y(step).wait()
-    largest = jnp.max(tops_y[...], axis=0)
+    for step in range(1, 2 * zs):
+        send_top(step).wait()
+    largest = jnp.max(tops[...], axis=0)
     gain_ref[...] = (line[:, :LANES] / (largest + 1e-6))[:, :rows * GROUP]
 
 
@@ -405,13 +426,13 @@
         scratch_shapes=[
             pltpu.SMEM((1, QUERIES), jnp.int32), pltpu.VMEM((8, LANES), F32), pltpu.VMEM((8, LANES), jnp.int32),
             pltpu.VMEM((8, LANES), jnp.int32), pltpu.VMEM((here, docs), jnp.int32),
-            pltpu.VMEM((3, 24, LANES), F32), pltpu.VMEM((3, 24, LANES, LANES), F32), pltpu.VMEM((feats, 16, LANES), BF16),
+            pltpu.VMEM((3, 24, LANES), F32), pltpu.VMEM((3, 25, LANES, LANES), F32), pltpu.VMEM((feats, 16, LANES), BF16),
             pltpu.VMEM((2, 16, 1024), BF16), pltpu.VMEM((4, BINS, BINS), BF16),
             pltpu.VMEM((groups, 2 * HIGH, BINS), F32), pltpu.VMEM((rows, 2 * HIGH, BINS), F32),
-            pltpu.VMEM((rows, GROUP, 2, BINS), F32), pltpu.VMEM((rows, 1, BINS), F32),
-            pltpu.VMEM((zs, 1, LANES), F32), pltpu.VMEM((ys, 1, LANES), F32),
-            dma((4,)), dma((groups,)), *pair(2), *pair(zs), *pair(ys),
-            *pair(rows), *pair(rows), *pair(zs), *pair(ys), *pair(rows),
+            pltpu.VMEM((rows, GROUP, 2, BINS), F32), pltpu.VMEM((2 * rows, 1, BINS), F32),
+            pltpu.VMEM((2 * zs, 1, LANES), F32),
+            dma((4,)), dma((ys,)), *pair(2), *pair(zs), *pair(ys),
+            *pair(rows), *pair(2 * rows), *pair(2 * zs), *pair(rows),
         ],
         compiler_params=pltpu.CompilerParams(collective_id=0, has_side_effects=True, vmem_limit_bytes=60 * 2 ** 20),
         name="round",

time: 59.6 us -> 58.7 us (0.985)
  Pallas kernels: 58.8 us -> 58 us
    pallas_call x1, Pallas kernels: 58.1 us -> 57.3 us  [one_round(): pl.pallas_call(functools.partial(round_kernel, rows, ys, zs), out_shape=(...]
where the time goes in v3:
time: 58.7 us; the launch traced here: 58.6 us
  Pallas kernels  58 us (99%)
  between operations  0.64 us (1%)
    pallas_call x1, Pallas kernels, one_round(): pl.pallas_call(functools.partial(round_kernel, rows, ys, zs), out_shape=(...  57.3 us

profile of v3, /device:TPU:1, one launch (start us, length us, event | category | flops | bytes accessed | tf_op | source)
XLA Modules:
  0.0 58.6 jit_solution(18299773777997942584)
XLA Ops:
  0.6 57.3 %round.1 = (f32[8,128]{1,0:T(8,128)S(1)}, f32[8,128]{1,0:T(8,128)S(1)}, f32[64,2,256]{2,1,0:T(2,128)S(1)}, f32[1,64]{1,0:T(1,128)S(1)}) custom-call(s32[1,64]{1,0:T(1,128)} %refs_0_.1, f32[8,128]{1,0:T(8,128)} %bitcast.6, s32[8,128]{1,0:T(8,128)} %bitcast.7, s32[8,128]{1,0:T(8,128)} %bitcast.8, s32[64,32768]{1,0:T(8,128)} %refs_4_.1), custom_call_target="tpu_custom_call" | custom-call | tf_op jit(solution)/shard_map/round/pallas_call | solution.py:421
  57.9 0.7 %publish.1 = (f32[8,128]{1,0:T(8,128)}, f32[8,128]{1,0:T(8,128)}, f32[64,2,256]{2,1,0:T(2,128)}, f32[1,64]{1,0:T(1,128)}) custom-call(f32[8,128]{1,0:T(8,128)S(1)} %get-tuple-element.12.refs_0_, f32[8,128]{1,0:T(8,128)S(1)} %get-tuple-element.13.refs_1_, f32[64,2,256]{2,1,0:T(2,128)S(1)} %get-tuple-element.14.refs_2_, f32[1,64]{1,0:T(1,128)S(1)} %get-tuple-element.15.refs_3_), custom_call_target="tpu_custom_call" | custom-call | tf_op jit(solution)/shard_map/publish/pallas_call | solution.py:454

commit v4 on v3

--- a/solution.py
+++ b/solution.py
@@ -190,9 +190,6 @@
     own = (odds, gains, discs)
     for which in range(3):
         window[which, 8:16, :] = own[which]
-    for which, value in enumerate((0.0, -1.0, 0.0)):
-        wide[which, 24] = jnp.full((LANES, LANES), value, F32)
-    build_matrices(matrices)
     pl.semaphore_wait(barrier, 2 + 2 * zs - 1 + 1 + 2 * rows - 1)
     halos = []
     for side, (target, place) in enumerate(((feats - 1, 16), (1, 0))):
@@ -203,6 +200,9 @@
         copy.start()
         halos.append(copy)
     code_load(0).start()
+    for which, value in enumerate((0.0, -1.0, 0.0)):
+        wide[which, 24] = jnp.full((LANES, LANES), value, F32)
+    build_matrices(matrices)
     first, count = query_spans(tiles_ref, feat)
     widen(window, wide, 1)
     for copy in halos:
@@ -248,16 +248,68 @@
 
     zero = jnp.zeros((), BF16)
 
-    @pl.loop(0, chunks)
+    def arrived(offset):
+        over_z(zs - offset).wait_recv()
+
+    def owner_of(turn):
+        inner = lax.rem(turn, zs)
+        odd = lax.rem(inner, 2)
+        offset = odd * ((inner + 1) // 2) + (1 - odd) * (zs - inner // 2)
+        outer = turn // zs
+        owner_y = lax.rem(y_high + outer // 2, 2) * 2 + lax.rem(y_low + lax.rem(outer, 2), 2)
+        return owner_y * zs + lax.rem(z + offset, zs)
+
+    def add_chunks(owners):
+        for slot, owner in enumerate(owners):
+            part = gathered[owner].astype(F32)
+            for which in range(2):
+                for tile in range(8):
+                    line = which * 8 + tile
+                    at = slot * 1024 + tile * LANES
+                    spread[which, :, at:at + LANES] = jnp.broadcast_to(part[line:line + 1], (16, LANES)).astype(BF16)
+        for slot, owner in enumerate(owners):
+            for k in range(1024 // BINS):
+                at = pl.ds(pl.multiple_of(owner * 1024 + k * BINS, BINS), BINS)
+                there = slot * 1024 + k * BINS
+                lam = [spread[which, :, there:there + BINS] for which in range(2)]
+                for group in range(groups):
+                    code = codes[group * GROUP:(group + 1) * GROUP, at]
+                    high = (code >> 5).astype(F32)
+                    high = jnp.concatenate([high, high - 1.0], axis=0).astype(BF16)
+                    hits = [high == jnp.array(2 * k, BF16) for k in range(HIGH // 2)]
+                    lhs = jnp.concatenate([jnp.where(hit, value, zero) for value in lam for hit in hits], axis=0)
+                    low = code & (LOW - 1)
+                    low = jnp.concatenate([low - k for k in range(4)], axis=0).astype(I8)
+                    rhs = jnp.concatenate(
+                        [jnp.where(low == jnp.array(4 * k, I8), jnp.ones((), F8), jnp.zeros((), F8))
+                         for k in range(LOW // 4)], axis=0)
+                    stage = group // 2 % 2
+                    pltpu.matmul_push_rhs(rhs, stage, group % 2, transpose=True)
+                    pltpu.matmul_acc_lhs(accs[group], lhs, load_staged_rhs=stage)
+
+    @pl.loop(0, 2)
     def _(turn):
-        for at in range(1, 5):
-            @pl.when(turn == at)
-            def _():
-                for offset in offsets[at - 1:at] if at < 4 else offsets[at - 1:]:
-                    over_z(zs - offset).wait_recv()
-                if at == 4:
-                    for step in range(1, ys):
-                        over_y(step).start()
+        @pl.when(turn == 1)
+        def _():
+            arrived(offsets[0])
+
+        add_chunks([owner_of(turn)])
+
+    @pl.loop(0, (chunks - 2) // 2)
+    def _(pair):
+        turn = 2 * pair + 2
+
+        @pl.when(turn == 2)
+        def _():
+            for offset in offsets[1:3]:
+                arrived(offset)
+
+        @pl.when(turn == 4)
+        def _():
+            for offset in offsets[3:]:
+                arrived(offset)
+            for step in range(1, ys):
+                over_y(step).start()
 
         for step in range(1, ys):
             @pl.when(turn == step * zs)
@@ -265,35 +317,7 @@
                 over_y(step).wait_recv()
                 code_load(step).wait()
 
-        inner = lax.rem(turn, zs)
-        odd = lax.rem(inner, 2)
-        offset = odd * ((inner + 1) // 2) + (1 - odd) * (zs - inner // 2)
-        outer = turn // zs
-        owner_y = lax.rem(y_high + outer // 2, 2) * 2 + lax.rem(y_low + lax.rem(outer, 2), 2)
-        owner = owner_y * zs + lax.rem(z + offset, zs)
-        part = gathered[owner].astype(F32)
-        for which in range(2):
-            for tile in range(8):
-                line = which * 8 + tile
-                spread[which, :, tile * LANES:(tile + 1) * LANES] = jnp.broadcast_to(
-                    part[line:line + 1], (16, LANES)).astype(BF16)
-        for k in range(1024 // BINS):
-            at = pl.ds(pl.multiple_of(owner * 1024 + k * BINS, BINS), BINS)
-            lam = [spread[which, :, k * BINS:(k + 1) * BINS] for which in range(2)]
-            for group in range(groups):
-                code = codes[group * GROUP:(group + 1) * GROUP, at]
-                high = (code >> 5).astype(F32)
-                high = jnp.concatenate([high, high - 1.0], axis=0).astype(BF16)
-                hits = [high == jnp.array(2 * k, BF16) for k in range(HIGH // 2)]
-                lhs = jnp.concatenate([jnp.where(hit, value, zero) for value in lam for hit in hits], axis=0)
-                low = code & (LOW - 1)
-                low = jnp.concatenate([low - k for k in range(4)], axis=0).astype(I8)
-                rhs = jnp.concatenate(
-                    [jnp.where(low == jnp.array(4 * k, I8), jnp.ones((), F8), jnp.zeros((), F8))
-                     for k in range(LOW // 4)], axis=0)
-                stage = group // 2 % 2
-                pltpu.matmul_push_rhs(rhs, stage, group % 2, transpose=True)
-                pltpu.matmul_acc_lhs(accs[group], lhs, load_staged_rhs=stage)
+        add_chunks([owner_of(turn), owner_of(turn + 1)])
 
     shape = (2 * HIGH, GROUP, BINS)
     same = iota(shape, 1) == (iota(shape, 2) & (GROUP - 1))
@@ -427,7 +451,7 @@
             pltpu.SMEM((1, QUERIES), jnp.int32), pltpu.VMEM((8, LANES), F32), pltpu.VMEM((8, LANES), jnp.int32),
             pltpu.VMEM((8, LANES), jnp.int32), pltpu.VMEM((here, docs), jnp.int32),
             pltpu.VMEM((3, 24, LANES), F32), pltpu.VMEM((3, 25, LANES, LANES), F32), pltpu.VMEM((feats, 16, LANES), BF16),
-            pltpu.VMEM((2, 16, 1024), BF16), pltpu.VMEM((4, BINS, BINS), BF16),
+            pltpu.VMEM((2, 16, 2048), BF16), pltpu.VMEM((4, BINS, BINS), BF16),
             pltpu.VMEM((groups, 2 * HIGH, BINS), F32), pltpu.VMEM((rows, 2 * HIGH, BINS), F32),
             pltpu.VMEM((rows, GROUP, 2, BINS), F32), pltpu.VMEM((2 * rows, 1, BINS), F32),
             pltpu.VMEM((2 * zs, 1, LANES), F32),

time: 58.7 us -> 56.8 us (0.968)
  Pallas kernels: 58 us -> 56.1 us
    pallas_call x1, Pallas kernels: 57.3 us -> 55.4 us  [one_round(): pl.pallas_call(functools.partial(round_kernel, rows, ys, zs), out_shape=(...]
where the time goes in v4:
time: 56.8 us; the launch traced here: 56.7 us
  Pallas kernels  56.1 us (99%)
  between operations  0.64 us (1%)
    pallas_call x1, Pallas kernels, one_round(): pl.pallas_call(functools.partial(round_kernel, rows, ys, zs), out_shape=(...  55.4 us

profile of v4, /device:TPU:1, one launch (start us, length us, event | category | flops | bytes accessed | tf_op | source)
XLA Modules:
  0.0 56.7 jit_solution(11557315314915160020)
XLA Ops:
  0.6 55.4 %round.1 = (f32[8,128]{1,0:T(8,128)S(1)}, f32[8,128]{1,0:T(8,128)S(1)}, f32[64,2,256]{2,1,0:T(2,128)S(1)}, f32[1,64]{1,0:T(1,128)S(1)}) custom-call(s32[1,64]{1,0:T(1,128)} %refs_0_.1, f32[8,128]{1,0:T(8,128)} %bitcast.6, s32[8,128]{1,0:T(8,128)} %bitcast.7, s32[8,128]{1,0:T(8,128)} %bitcast.8, s32[64,32768]{1,0:T(8,128)} %refs_4_.1), custom_call_target="tpu_custom_call" | custom-call | tf_op jit(solution)/shard_map/round/pallas_call | solution.py:445
  56.0 0.7 %publish.1 = (f32[8,128]{1,0:T(8,128)}, f32[8,128]{1,0:T(8,128)}, f32[64,2,256]{2,1,0:T(2,128)}, f32[1,64]{1,0:T(1,128)}) custom-call(f32[8,128]{1,0:T(8,128)S(1)} %get-tuple-element.12.refs_0_, f32[8,128]{1,0:T(8,128)S(1)} %get-tuple-element.13.refs_1_, f32[64,2,256]{2,1,0:T(2,128)S(1)} %get-tuple-element.14.refs_2_, f32[1,64]{1,0:T(1,128)S(1)} %get-tuple-element.15.refs_3_), custom_call_target="tpu_custom_call" | custom-call | tf_op jit(solution)/shard_map/publish/pallas_call | solution.py:478

commit v5 on v4

--- a/solution.py
+++ b/solution.py
@@ -48,13 +48,16 @@
     return place, 1.0 / jnp.log2(place + 2.0)
 
 
-def query_scale(window, first, count):
-    place, table = discount_table()
+def span_rows(first, count):
     rows = iota((8, LANES), 0)
     first_rows, count_rows = jnp.zeros((8, LANES), jnp.int32), jnp.zeros((8, LANES), jnp.int32)
     for tile in range(8):
         first_rows = jnp.where(rows == tile, first[tile], first_rows)
         count_rows = jnp.where(rows == tile, count[tile], count_rows)
+    return first_rows, count_rows
+
+
+def query_scale(window, first_rows, count_rows, place, table):
     all_gains = window[1]
     reach = jnp.concatenate([(all_gains >= F32(2 ** level - 1)).astype(F32) for level in range(1, 5)], axis=0)
     reach = jnp.broadcast_to(jnp.sum(reach, axis=1, keepdims=True), (96, LANES))
@@ -102,7 +105,7 @@
             return grad, hess
 
         empty = jnp.zeros((rows, LANES), F32)
-        grad, hess = lax.fori_loop(0, MAX_TILES, column, (empty, empty))
+        grad, hess = lax.fori_loop(0, MAX_TILES, column, (empty, empty), unroll=4)
         grads.append(jnp.sum(grad, axis=0, keepdims=True))
         hessians.append(jnp.sum(hess, axis=0, keepdims=True))
     return jnp.concatenate(grads, axis=0), jnp.concatenate(hessians, axis=0)
@@ -204,6 +207,8 @@
         wide[which, 24] = jnp.full((LANES, LANES), value, F32)
     build_matrices(matrices)
     first, count = query_spans(tiles_ref, feat)
+    span = span_rows(first, count)
+    place, table = discount_table()
     widen(window, wide, 1)
     for copy in halos:
         copy.wait()
@@ -211,7 +216,7 @@
         code_load(step).start()
     widen(window, wide, 0)
     widen(window, wide, 2)
-    scale = query_scale(window, first, count)
+    scale = query_scale(window, *span, place, table)
     grad, hess = pair_sums(own, wide, first, count)
     grad = -grad * scale
     hess = hess * (odds * scale)
@@ -295,29 +300,24 @@
 
         add_chunks([owner_of(turn)])
 
-    @pl.loop(0, (chunks - 2) // 2)
-    def _(pair):
-        turn = 2 * pair + 2
-
-        @pl.when(turn == 2)
-        def _():
-            for offset in offsets[1:3]:
-                arrived(offset)
-
-        @pl.when(turn == 4)
-        def _():
-            for offset in offsets[3:]:
-                arrived(offset)
-            for step in range(1, ys):
-                over_y(step).start()
-
+    for offset in offsets[1:3]:
+        arrived(offset)
+    add_chunks([owner_of(jnp.int32(turn)) for turn in (2, 3)])
+    for offset in offsets[3:]:
+        arrived(offset)
+    for step in range(1, ys):
+        over_y(step).start()
+
+    @pl.loop(1, chunks // 4)
+    def _(four):
+        turn = 4 * four
         for step in range(1, ys):
             @pl.when(turn == step * zs)
             def _():
                 over_y(step).wait_recv()
                 code_load(step).wait()
 
-        add_chunks([owner_of(turn), owner_of(turn + 1)])
+        add_chunks([owner_of(turn + k) for k in range(4)])
 
     shape = (2 * HIGH, GROUP, BINS)
     same = iota(shape, 1) == (iota(shape, 2) & (GROUP - 1))
@@ -451,7 +451,7 @@
             pltpu.SMEM((1, QUERIES), jnp.int32), pltpu.VMEM((8, LANES), F32), pltpu.VMEM((8, LANES), jnp.int32),
             pltpu.VMEM((8, LANES), jnp.int32), pltpu.VMEM((here, docs), jnp.int32),
             pltpu.VMEM((3, 24, LANES), F32), pltpu.VMEM((3, 25, LANES, LANES), F32), pltpu.VMEM((feats, 16, LANES), BF16),
-            pltpu.VMEM((2, 16, 2048), BF16), pltpu.VMEM((4, BINS, BINS), BF16),
+            pltpu.VMEM((2, 16, 4096), BF16), pltpu.VMEM((4, BINS, BINS), BF16),
             pltpu.VMEM((groups, 2 * HIGH, BINS), F32), pltpu.VMEM((rows, 2 * HIGH, BINS), F32),
             pltpu.VMEM((rows, GROUP, 2, BINS), F32), pltpu.VMEM((2 * rows, 1, BINS), F32),
             pltpu.VMEM((2 * zs, 1, LANES), F32),

time: 56.8 us -> 55.4 us (0.975)
  Pallas kernels: 56.1 us -> 54.7 us
    pallas_call x1, Pallas kernels: 55.4 us -> 54 us  [one_round(): pl.pallas_call(functools.partial(round_kernel, rows, ys, zs), out_shape=(...]
where the time goes in v5:
time: 55.4 us; the launch traced here: 55.3 us
  Pallas kernels  54.7 us (99%)
  between operations  0.64 us (1%)
    pallas_call x1, Pallas kernels, one_round(): pl.pallas_call(functools.partial(round_kernel, rows, ys, zs), out_shape=(...  54 us

profile of v5, /device:TPU:1, one launch (start us, length us, event | category | flops | bytes accessed | tf_op | source)
XLA Modules:
  0.0 55.3 jit_solution(6076313503350344877)
XLA Ops:
  0.6 54.0 %round.1 = (f32[8,128]{1,0:T(8,128)S(1)}, f32[8,128]{1,0:T(8,128)S(1)}, f32[64,2,256]{2,1,0:T(2,128)S(1)}, f32[1,64]{1,0:T(1,128)S(1)}) custom-call(s32[1,64]{1,0:T(1,128)} %refs_0_.1, f32[8,128]{1,0:T(8,128)} %bitcast.6, s32[8,128]{1,0:T(8,128)} %bitcast.7, s32[8,128]{1,0:T(8,128)} %bitcast.8, s32[64,32768]{1,0:T(8,128)} %refs_4_.1), custom_call_target="tpu_custom_call" | custom-call | tf_op jit(solution)/shard_map/round/pallas_call | solution.py:445
  54.6 0.7 %publish.1 = (f32[8,128]{1,0:T(8,128)}, f32[8,128]{1,0:T(8,128)}, f32[64,2,256]{2,1,0:T(2,128)}, f32[1,64]{1,0:T(1,128)}) custom-call(f32[8,128]{1,0:T(8,128)S(1)} %get-tuple-element.12.refs_0_, f32[8,128]{1,0:T(8,128)S(1)} %get-tuple-element.13.refs_1_, f32[64,2,256]{2,1,0:T(2,128)S(1)} %get-tuple-element.14.refs_2_, f32[1,64]{1,0:T(1,128)S(1)} %get-tuple-element.15.refs_3_), custom_call_target="tpu_custom_call" | custom-call | tf_op jit(solution)/shard_map/publish/pallas_call | solution.py:478

commit v6 on v5

--- a/solution.py
+++ b/solution.py
@@ -105,7 +105,7 @@
             return grad, hess
 
         empty = jnp.zeros((rows, LANES), F32)
-        grad, hess = lax.fori_loop(0, MAX_TILES, column, (empty, empty), unroll=4)
+        grad, hess = lax.fori_loop(0, MAX_TILES, column, (empty, empty), unroll=8)
         grads.append(jnp.sum(grad, axis=0, keepdims=True))
         hessians.append(jnp.sum(hess, axis=0, keepdims=True))
     return jnp.concatenate(grads, axis=0), jnp.concatenate(hessians, axis=0)
@@ -124,7 +124,7 @@
 
 def round_kernel(rows, ys, zs, *refs):
     accumulators = ([pltpu.ACC(k % 2)((2 * HIGH * GROUP, BINS), F32) for k in range(rows)]
-                    + [pltpu.ACC(k % 2)((48, BINS), F32) for k in range(3)] + [pltpu.ACC(0)((32, BINS), F32)])
+                    + [pltpu.ACC(mxu)((48, BINS), F32) for mxu in (0, 0, 1)] + [pltpu.ACC(1)((32, BINS), F32)])
     pl.run_scoped(lambda *accs: round_body(rows, ys, zs, accs[:rows], accs[rows:], *refs), *accumulators)
 
 
@@ -321,15 +321,17 @@
 
     shape = (2 * HIGH, GROUP, BINS)
     same = iota(shape, 1) == (iota(shape, 2) & (GROUP - 1))
-    for group in range(groups):
-        total = pltpu.matmul_pop(accs[group]).reshape(shape)
-        mine[group] = jnp.sum(jnp.where(same, total, 0.0), axis=1)
-
-        @pl.when(row != group)
-        def _():
-            scatter(group).start()
-
-
+    for batch in range(0, groups, 4):
+        for group in range(batch, batch + 4):
+            total = pltpu.matmul_pop(accs[group]).reshape(shape)
+            mine[group] = jnp.sum(jnp.where(same, total, 0.0), axis=1)
+        for group in range(batch, batch + 4):
+            @pl.when(row != group)
+            def _():
+                scatter(group).start()
+
+    for k, mxu, stage in ((1, 0, 0), (2, 1, 0), (0, 0, 1), (3, 1, 1)):
+        pltpu.matmul_push_rhs(matrices[k], stage, mxu)
     for step in range(1, zs):
         over_z(step).wait_send()
     for step in range(1, ys):
@@ -342,9 +344,8 @@
         summed = summed + parts[k]
 
     split = jnp.concatenate(pieces(summed), axis=0)
-    for k in range(3):
-        pltpu.matmul_push_rhs(matrices[k], k // 2, k % 2)
-        pltpu.matmul_acc_lhs(small[k], split, load_staged_rhs=k // 2)
+    for k, stage in ((1, 0), (2, 0), (0, 1)):
+        pltpu.matmul_acc_lhs(small[k], split, load_staged_rhs=stage)
 
     def product(k):
         full = pltpu.matmul_pop(small[k])
@@ -413,8 +414,7 @@
         every = jnp.maximum(every, pltpu.roll(every, BINS - shift, 1))
     every = jnp.where((iota((rows, BINS), 1) & (LOW - 1)) == 0, every, 0.0)
     split = jnp.concatenate([piece.astype(F32) for piece in pieces(every)] + [jnp.zeros((rows, BINS), F32)], axis=0)
-    pltpu.matmul_push_rhs(matrices[3], 0, 0)
-    pltpu.matmul_acc_lhs(small[3], split.astype(BF16), load_staged_rhs=0)
+    pltpu.matmul_acc_lhs(small[3], split.astype(BF16), load_staged_rhs=1)
     full = pltpu.matmul_pop(small[3])
     chosen = full[0:rows] + (full[rows:2 * rows] + full[2 * rows:3 * rows])
     owned = (iota((rows, BINS), 1) >> 3) == iota((rows, BINS), 0)

time: 55.4 us -> 55.2 us (level)
  no operation moved by 1% of the time
where the time goes in v6:
time: 55.2 us; the launch traced here: 55.1 us
  Pallas kernels  54.4 us (99%)
  between operations  0.64 us (1%)
    pallas_call x1, Pallas kernels, one_round(): pl.pallas_call(functools.partial(round_kernel, rows, ys, zs), out_shape=(...  53.7 us

profile of v6, /device:TPU:1, one launch (start us, length us, event | category | flops | bytes accessed | tf_op | source)
XLA Modules:
  0.0 55.1 jit_solution(10373906262030126184)
XLA Ops:
  0.6 53.7 %round.1 = (f32[8,128]{1,0:T(8,128)S(1)}, f32[8,128]{1,0:T(8,128)S(1)}, f32[64,2,256]{2,1,0:T(2,128)S(1)}, f32[1,64]{1,0:T(1,128)S(1)}) custom-call(s32[1,64]{1,0:T(1,128)} %refs_0_.1, f32[8,128]{1,0:T(8,128)} %bitcast.6, s32[8,128]{1,0:T(8,128)} %bitcast.7, s32[8,128]{1,0:T(8,128)} %bitcast.8, s32[64,32768]{1,0:T(8,128)} %refs_4_.1), custom_call_target="tpu_custom_call" | custom-call | tf_op jit(solution)/shard_map/round/pallas_call | solution.py:445
  54.3 0.7 %publish.1 = (f32[8,128]{1,0:T(8,128)}, f32[8,128]{1,0:T(8,128)}, f32[64,2,256]{2,1,0:T(2,128)}, f32[1,64]{1,0:T(1,128)}) custom-call(f32[8,128]{1,0:T(8,128)S(1)} %get-tuple-element.12.refs_0_, f32[8,128]{1,0:T(8,128)S(1)} %get-tuple-element.13.refs_1_, f32[64,2,256]{2,1,0:T(2,128)S(1)} %get-tuple-element.14.refs_2_, f32[1,64]{1,0:T(1,128)S(1)} %get-tuple-element.15.refs_3_), custom_call_target="tpu_custom_call" | custom-call | tf_op jit(solution)/shard_map/publish/pallas_call | solution.py:478

commit v7 on v6

--- a/solution.py
+++ b/solution.py
@@ -212,8 +212,7 @@
     widen(window, wide, 1)
     for copy in halos:
         copy.wait()
-    for step in range(1, ys):
-        code_load(step).start()
+    code_load(1).start()
     widen(window, wide, 0)
     widen(window, wide, 2)
     scale = query_scale(window, *span, place, table)
@@ -288,9 +287,8 @@
                     rhs = jnp.concatenate(
                         [jnp.where(low == jnp.array(4 * k, I8), jnp.ones((), F8), jnp.zeros((), F8))
                          for k in range(LOW // 4)], axis=0)
-                    stage = group // 2 % 2
-                    pltpu.matmul_push_rhs(rhs, stage, group % 2, transpose=True)
-                    pltpu.matmul_acc_lhs(accs[group], lhs, load_staged_rhs=stage)
+                    pltpu.matmul_push_rhs(rhs, 0, group % 2, transpose=True)
+                    pltpu.matmul_acc_lhs(accs[group], lhs, load_staged_rhs=0)
 
     @pl.loop(0, 2)
     def _(turn):
@@ -307,6 +305,8 @@
         arrived(offset)
     for step in range(1, ys):
         over_y(step).start()
+    for step in range(2, ys):
+        code_load(step).start()
 
     @pl.loop(1, chunks // 4)
     def _(four):

time: 55.2 us -> 55 us (level)
  no operation moved by 1% of the time
where the time goes in v7:
time: 55 us; the launch traced here: 54.9 us
  Pallas kernels  54.2 us (99%)
  between operations  0.64 us (1%)
    pallas_call x1, Pallas kernels, one_round(): pl.pallas_call(functools.partial(round_kernel, rows, ys, zs), out_shape=(...  53.5 us

profile of v7, /device:TPU:1, one launch (start us, length us, event | category | flops | bytes accessed | tf_op | source)
XLA Modules:
  0.0 54.9 jit_solution(17893801145501704862)
XLA Ops:
  0.6 53.5 %round.1 = (f32[8,128]{1,0:T(8,128)S(1)}, f32[8,128]{1,0:T(8,128)S(1)}, f32[64,2,256]{2,1,0:T(2,128)S(1)}, f32[1,64]{1,0:T(1,128)S(1)}) custom-call(s32[1,64]{1,0:T(1,128)} %refs_0_.1, f32[8,128]{1,0:T(8,128)} %bitcast.6, s32[8,128]{1,0:T(8,128)} %bitcast.7, s32[8,128]{1,0:T(8,128)} %bitcast.8, s32[64,32768]{1,0:T(8,128)} %refs_4_.1), custom_call_target="tpu_custom_call" | custom-call | tf_op jit(solution)/shard_map/round/pallas_call | solution.py:445
  54.2 0.7 %publish.1 = (f32[8,128]{1,0:T(8,128)}, f32[8,128]{1,0:T(8,128)}, f32[64,2,256]{2,1,0:T(2,128)}, f32[1,64]{1,0:T(1,128)}) custom-call(f32[8,128]{1,0:T(8,128)S(1)} %get-tuple-element.12.refs_0_, f32[8,128]{1,0:T(8,128)S(1)} %get-tuple-element.13.refs_1_, f32[64,2,256]{2,1,0:T(2,128)S(1)} %get-tuple-element.14.refs_2_, f32[1,64]{1,0:T(1,128)S(1)} %get-tuple-element.15.refs_3_), custom_call_target="tpu_custom_call" | custom-call | tf_op jit(solution)/shard_map/publish/pallas_call | solution.py:478

commit v8 on v7

--- a/solution.py
+++ b/solution.py
@@ -212,7 +212,8 @@
     widen(window, wide, 1)
     for copy in halos:
         copy.wait()
-    code_load(1).start()
+    for step in range(1, ys):
+        code_load(step).start()
     widen(window, wide, 0)
     widen(window, wide, 2)
     scale = query_scale(window, *span, place, table)
@@ -305,8 +306,6 @@
         arrived(offset)
     for step in range(1, ys):
         over_y(step).start()
-    for step in range(2, ys):
-        code_load(step).start()
 
     @pl.loop(1, chunks // 4)
     def _(four):

time: 55 us -> 55 us (level)
  no operation moved by 1% of the time
where the time goes in v8:
time: 55 us; the launch traced here: 54.9 us
  Pallas kernels  54.2 us (99%)
  between operations  0.64 us (1%)
    pallas_call x1, Pallas kernels, one_round(): pl.pallas_call(functools.partial(round_kernel, rows, ys, zs), out_shape=(...  53.5 us

profile of v8, /device:TPU:1, one launch (start us, length us, event | category | flops | bytes accessed | tf_op | source)
XLA Modules:
  0.0 54.9 jit_solution(7014257155468303036)
XLA Ops:
  0.6 53.5 %round.1 = (f32[8,128]{1,0:T(8,128)S(1)}, f32[8,128]{1,0:T(8,128)S(1)}, f32[64,2,256]{2,1,0:T(2,128)S(1)}, f32[1,64]{1,0:T(1,128)S(1)}) custom-call(s32[1,64]{1,0:T(1,128)} %refs_0_.1, f32[8,128]{1,0:T(8,128)} %bitcast.6, s32[8,128]{1,0:T(8,128)} %bitcast.7, s32[8,128]{1,0:T(8,128)} %bitcast.8, s32[64,32768]{1,0:T(8,128)} %refs_4_.1), custom_call_target="tpu_custom_call" | custom-call | tf_op jit(solution)/shard_map/round/pallas_call | solution.py:444
  54.2 0.7 %publish.1 = (f32[8,128]{1,0:T(8,128)}, f32[8,128]{1,0:T(8,128)}, f32[64,2,256]{2,1,0:T(2,128)}, f32[1,64]{1,0:T(1,128)}) custom-call(f32[8,128]{1,0:T(8,128)S(1)} %get-tuple-element.12.refs_0_, f32[8,128]{1,0:T(8,128)S(1)} %get-tuple-element.13.refs_1_, f32[64,2,256]{2,1,0:T(2,128)S(1)} %get-tuple-element.14.refs_2_, f32[1,64]{1,0:T(1,128)S(1)} %get-tuple-element.15.refs_3_), custom_call_target="tpu_custom_call" | custom-call | tf_op jit(solution)/shard_map/publish/pallas_call | solution.py:477
